TPU v7x, 256 devices: a whole 4x4x8 slice. The times are simulated.
256 devices in a mesh: grp: 8 (over z_lo, core), tm: 32 (over z_hi, y, x).
Axes of the slice: x: 4, y: 4, z: 8 (z_hi: 2, z_lo: 4; z = z_hi * 4 + z_lo), core: 2. Of those that a mesh axis runs over, the one named last changes fastest.
Arguments:
- x_start: float32 [4096, 128], P(('grp', 'tm')), may hold values from -3 to 3
- y_start: float32 [1024, 128], P('tm'), may hold values from 0 to 1
- cost: float32 [4096, 128], P(('grp', 'tm')), may hold values from -6 to 6
- rhs: float32 [1024, 128], P('tm'), may hold values from -6 to 6
- tiles: float32 [16384, 128, 128], P(('grp', 'tm')), may hold values from -0.1875 to 0.1875
- tile_rows: int32 [16384], P(('grp', 'tm')), may hold values from 0 to 1023, as said below
- tile_cols: int32 [16384], P(('grp', 'tm')), may hold values from 0 to 4095, as said below
- tile_count: int32 [256], P(('grp', 'tm')), may hold values from 1 to 64, as said below
- var_class: int32 [4096, 128], P(('grp', 'tm')), may hold values from 0 to 7
- lower_table: float32 [8], replicated, may hold values from -1 to -0.2
- upper_table: float32 [8], replicated, may hold values from 0.2 to 1
Outputs:
- primal: float32 [4096, 128], P(('grp', 'tm'))
- dual: float32 [1024, 128], P('tm')
- primal_mean: float32 [4096, 128], P(('grp', 'tm'))
- dual_mean: float32 [1024, 128], P('tm')
Inputs may be any that keep to these rules, and one draw needn't show every extreme that they name: `tile_cols`: the tile slots of device d (slots d * 64 to (d + 1) * 64 - 1) name only that device's own column blocks d * 16 to (d + 1) * 16 - 1. `tile_rows`: the tile slots of device d = g * 32 + t name only row blocks of time blocks t - 1, t and t + 1 (rows k * 32 to (k + 1) * 32 - 1 belong to time block k). Only the first tile_count[d] slots of device d are live; some device has all 64 slots live.
All inputs are finite; a program needn't handle non-finite values.
Results may differ from a plain program's by a relative error of at most 0.0001.
Values sent between devices are 32-bit elements; how exact they have to be, the bound alone decides.
A program may use at most 64 MiB of HBM per device.

v0:
```python
import jax
import jax.numpy as jnp
from jax import lax
from jax.sharding import PartitionSpec as P

ITERS = 2


primal_step = 0.6
dual_step = 0.6


def with_halo(block, sides, width):
    for axis, dim in sides:
        count = lax.axis_size(axis)
        forward = [(i, i + 1) for i in range(count - 1)]
        backward = [(target, source) for source, target in forward]
        low = lax.ppermute(
            lax.slice_in_dim(block, block.shape[dim] - width, None, axis=dim), axis, forward
        )
        high = lax.ppermute(lax.slice_in_dim(block, 0, width, axis=dim), axis, backward)
        block = jnp.concatenate([low, block, high], axis=dim)
    return block


def shifted(block, axis, distance):
    devices = range(lax.axis_size(axis))
    route = [(i - distance, i) for i in devices if i - distance in devices]
    return lax.ppermute(block, axis, route)


def dual_update(dual_part, rhs_part, image_part):
    return jnp.maximum(dual_part + dual_step * (rhs_part - image_part), 0.0)


def body(
    x_start,
    y_start,
    cost,
    rhs,
    tiles,
    tile_rows,
    tile_cols,
    tile_count,
    var_class,
    lower_table,
    upper_table,
):
    tile_total = tiles.shape[0]
    col_blocks = x_start.shape[0]
    row_blocks = y_start.shape[0]
    time_devices = lax.axis_size("tm")
    time_index = lax.axis_index("tm")
    device_index = lax.axis_index("grp") * time_devices + time_index
    local_cols = tile_cols - device_index * col_blocks
    live_mask = (jnp.arange(tile_total) < tile_count[0]).astype(jnp.float32)[:, None]
    col_select = (local_cols[:, None] == jnp.arange(col_blocks)[None, :]).astype(jnp.float32)
    lower_bound = jnp.zeros(x_start.shape, jnp.float32)
    upper_bound = jnp.zeros(x_start.shape, jnp.float32)
    for class_id in range(lower_table.shape[0]):
        lower_bound = jnp.where(var_class == class_id, lower_table[class_id], lower_bound)
        upper_bound = jnp.where(var_class == class_id, upper_table[class_id], upper_bound)
    window_first = (time_index - 1) * row_blocks
    row_select = (
        (tile_rows - window_first)[:, None] == jnp.arange(3 * row_blocks)[None, :]
    ).astype(jnp.float32)
    dual_view = with_halo(y_start, (("tm", 0),), row_blocks)
    primal = x_start
    dual = y_start
    primal_total = jnp.zeros_like(x_start)
    dual_total = jnp.zeros_like(y_start)
    for iteration in range(ITERS):
        dual_picked = jnp.dot(row_select, dual_view, precision=lax.Precision.HIGHEST)
        backward = (
            jnp.einsum("nrc,nr->nc", tiles, dual_picked, precision=lax.Precision.HIGHEST)
            * live_mask
        )
        adjoint_part = jnp.dot(col_select.T, backward, precision=lax.Precision.HIGHEST)
        moved = primal - primal_step * (cost - adjoint_part)
        primal_next = jnp.minimum(jnp.maximum(moved, lower_bound), upper_bound)
        extrapolated = 2.0 * primal_next - primal
        primal_picked = jnp.dot(col_select, extrapolated, precision=lax.Precision.HIGHEST)
        forward = (
            jnp.einsum("nrc,nc->nr", tiles, primal_picked, precision=lax.Precision.HIGHEST)
            * live_mask
        )
        window_terms = jnp.dot(row_select.T, forward, precision=lax.Precision.HIGHEST)
        summed = lax.psum(window_terms, "grp")
        from_above = shifted(summed[:row_blocks], "tm", -1)
        from_below = shifted(summed[2 * row_blocks :], "tm", 1)
        image_slab = summed[row_blocks : 2 * row_blocks] + from_above + from_below
        dual_next = dual_update(dual, rhs, image_slab)
        if iteration + 1 < ITERS:
            dual_view = with_halo(dual_next, (("tm", 0),), row_blocks)
        primal_total = primal_total + primal_next
        dual_total = dual_total + dual_next
        primal = primal_next
        dual = dual_next
    return (primal, dual, primal_total / ITERS, dual_total / ITERS)


def solution(mesh):
    return jax.shard_map(
        body,
        mesh=mesh,
        in_specs=(
            P(("grp", "tm"), None),
            P("tm", None),
            P(("grp", "tm"), None),
            P("tm", None),
            P(("grp", "tm"), None, None),
            P(("grp", "tm")),
            P(("grp", "tm")),
            P(("grp", "tm")),
            P(("grp", "tm"), None),
            P(),
            P(),
        ),
        out_specs=(P(("grp", "tm"), None), P("tm", None), P(("grp", "tm"), None), P("tm", None)),
        check_vma=False,
    )
```

profile of v0, /device:TPU:128, one launch (start us, length us, event | category | flops | bytes accessed | tf_op | source)
XLA Modules:
  0.0 176.0 jit_solution(1812042930562841900)
XLA Ops:
  0.7 5.4 %collective-permute-start.1 = (f32[32,128]{1,0:T(8,128)}, f32[32,128]{1,0:T(8,128)S(1)}, u32[]{:S(2)}, u32[]{:S(2)}) collective-permute-start(f32[32,128]{1,0:T(8,128)} %param.12), channel_id=1, source_target_pairs={{1,0},{2,1},{3,2},{4,3},{5,4},{6,5},{7,6},{8,7},{9,8},{10,9},{11,1... | collective-permute-start | bytes 49160 | tf_op jit(solution)/shard_map/ppermute | solution.py:21
  6.1 1.9 %collective-permute-start = (f32[32,128]{1,0:T(8,128)}, f32[32,128]{1,0:T(8,128)S(1)}, u32[]{:S(2)}, u32[]{:S(2)}) collective-permute-start(f32[32,128]{1,0:T(8,128)} %param.12), channel_id=1, source_target_pairs={{0,1},{1,2},{2,3},{3,4},{4,5},{5,6},{6,7},{7,8},{8,9},{9,10},{10,1... | collective-permute-start | bytes 49160 | tf_op jit(solution)/shard_map/ppermute | solution.py:18
  8.7 1.6 fusion.64
  10.3 1.6 fusion.63
  11.9 0.7 broadcast_compare_fusion
  12.7 0.8 broadcast_subtract_fusion.1
  13.5 0.8 broadcast_subtract_fusion
  14.3 5.7 %collective-permute-done = f32[32,128]{1,0:T(8,128)S(1)} collective-permute-done((f32[32,128]{1,0:T(8,128)}, f32[32,128]{1,0:T(8,128)S(1)}, u32[]{:S(2)}, u32[]{:S(2)}) %collective-permute-start) | collective-permute-done | bytes 16416 | tf_op jit(solution)/shard_map/ppermute | solution.py:18
  20.1 0.9 fusion.8
  21.0 5.3 %fusion.65 = f32[64,1,128]{2,1,0:T(1,128)S(1)} fusion(f32[64,128,1]{1,2,0:T(1,128)S(1)} %bitcast.46, f32[64,128,128]{2,1,0:T(8,128)} %param.15), kind=kOutput, calls=%fused_computation.85 | convolution fusion | flops 12582912 | bytes 4259840 | tf_op jit(solution)/shard_map/nrc,nr->nc/dot_general | solution.py:75
  26.3 10.4 %fusion.7 = f32[16,128]{1,0:T(8,128)S(1)} fusion(f32[16,128]{1,0:T(8,128)S(1)} %copy-done.4, f32[16,128]{1,0:T(8,128)S(1)} %copy-done.5, f32[64,128]{1,0:T(8,128)S(1)} %bitcast.49, f32[64]{0:T(128)S(1)} %compare_convert_fusion, s32[64]{0:T(128)S(1)} %broadcast_subtract_fusion.1, pred[16,128]{1,0:T(8,128)(4,1)S(1)} %get-tuple-element.16, ...), kind=kOutput, calls=%fused_computation.9 | convolution fusion | flops 1625088 | bytes 74304 | tf_op jit(solution)/shard_map/dot_general | solution.py:78
  36.7 0.2 fusion.27
  37.0 6.6 %fusion.66 = f32[64,1,128]{2,1,0:T(1,128)S(1)} fusion(f32[64,128,1]{1,2,0:T(1,128)S(1)} %bitcast.53, f32[64,128,128]{2,1,0:T(8,128)S(1)} %copy-done), kind=kOutput, calls=%fused_computation.86 | convolution fusion | flops 12582912 | bytes 4259840 | tf_op jit(solution)/shard_map/nrc,nc->nr/dot_general | solution.py:84
  43.6 0.3 fusion.23
  43.9 28.8 %psum.14 = f32[96,128]{1,0:T(8,128)S(1)} all-reduce(f32[96,128]{1,0:T(8,128)S(1)} %fusion.23), channel_id=1, replica_groups=mesh['grp'=8,'tm'=32] {'grp'}, use_global_device_ids=true, to_apply=%region_0.1 | all-reduce | flops 12288 | bytes 98304 | tf_op jit(solution)/shard_map/psum | solution.py:88
  72.8 7.4 %collective-permute-start.2 = (f32[32,128]{1,0:T(8,128)S(1)}, f32[32,128]{1,0:T(8,128)S(1)}, u32[]{:S(2)}, u32[]{:S(2)}) collective-permute-start(f32[32,128]{1,0:T(8,128)S(1)} %get-tuple-element.8), channel_id=1, source_target_pairs={{1,0},{2,1},{3,2},{4,3},{5,4},{6,5},{7,6},{8,7},{9,8},{10,9},{11,1... | collective-permute-start | bytes 49160 | tf_op jit(solution)/shard_map/ppermute | solution.py:29
  80.2 1.9 %collective-permute-start.3 = (f32[32,128]{1,0:T(8,128)S(1)}, f32[32,128]{1,0:T(8,128)S(1)}, u32[]{:S(2)}, u32[]{:S(2)}) collective-permute-start(f32[32,128]{1,0:T(8,128)S(1)} %get-tuple-element.9), channel_id=1, source_target_pairs={{0,1},{1,2},{2,3},{3,4},{4,5},{5,6},{6,7},{7,8},{8,9},{9,10},{10,1... | collective-permute-start | bytes 49160 | tf_op jit(solution)/shard_map/ppermute | solution.py:29
  82.2 11.8 %collective-permute-done.3 = f32[32,128]{1,0:T(8,128)S(1)} collective-permute-done((f32[32,128]{1,0:T(8,128)S(1)}, f32[32,128]{1,0:T(8,128)S(1)}, u32[]{:S(2)}, u32[]{:S(2)}) %collective-permute-start.3) | collective-permute-done | bytes 16416 | tf_op jit(solution)/shard_map/ppermute | solution.py:29
  94.0 1.9 %collective-permute-start.5 = (f32[32,128]{1,0:T(8,128)S(1)}, f32[32,128]{1,0:T(8,128)S(1)}, u32[]{:S(2)}, u32[]{:S(2)}) collective-permute-start(f32[32,128]{1,0:T(8,128)S(1)} %fusion.37), channel_id=1, source_target_pairs={{1,0},{2,1},{3,2},{4,3},{5,4},{6,5},{7,6},{8,7},{9,8},{10,9},{11,1... | collective-permute-start | bytes 49160 | tf_op jit(solution)/shard_map/ppermute | solution.py:21
  95.9 4.1 %collective-permute-start.4 = (f32[32,128]{1,0:T(8,128)S(1)}, f32[32,128]{1,0:T(8,128)S(1)}, u32[]{:S(2)}, u32[]{:S(2)}) collective-permute-start(f32[32,128]{1,0:T(8,128)S(1)} %fusion.37), channel_id=1, source_target_pairs={{0,1},{1,2},{2,3},{3,4},{4,5},{5,6},{6,7},{7,8},{8,9},{9,10},{10,1... | collective-permute-start | bytes 49160 | tf_op jit(solution)/shard_map/ppermute | solution.py:18
  100.0 9.6 %collective-permute-done.4 = f32[32,128]{1,0:T(8,128)S(1)} collective-permute-done((f32[32,128]{1,0:T(8,128)S(1)}, f32[32,128]{1,0:T(8,128)S(1)}, u32[]{:S(2)}, u32[]{:S(2)}) %collective-permute-start.4) | collective-permute-done | bytes 16416 | tf_op jit(solution)/shard_map/ppermute | solution.py:18
  109.7 0.2 fusion.14
  109.9 5.3 %fusion.67 = f32[64,1,128]{2,1,0:T(1,128)S(1)} fusion(f32[64,128,1]{1,2,0:T(1,128)S(1)} %bitcast.47, f32[64,128,128]{2,1,0:T(8,128)} %param.15), kind=kOutput, calls=%fused_computation.87 | convolution fusion | flops 12582912 | bytes 4259840 | tf_op jit(solution)/shard_map/nrc,nr->nc/dot_general | solution.py:75
  115.2 11.1 %add_multiply_fusion.1 = (f32[16,128]{1,0:T(8,128)}, f32[16,128]{1,0:T(8,128)S(1)}) fusion(f32[16,128]{1,0:T(8,128)S(1)} %fusion.7, pred[16,128]{1,0:T(8,128)(4,1)S(1)} %get-tuple-element.16, pred[16,128]{1,0:T(8,128)(4,1)S(1)} %get-tuple-element.15, pred[16,128]{1,0:T(8,128)(4,1)S(1)} %get-tuple-element.14, pred[16,128]{1,0:T(8,128)(4,1)S(1)} %get-tuple-element.13, ...), kind=kOutput, calls=%fused_computation.57 | convolution fusion | flops 1629184 | bytes 82496 | tf_op jit(solution)/shard_map/dot_general | solution.py:78
  126.2 0.2 fusion.26
  126.5 6.6 %fusion.68 = f32[64,1,128]{2,1,0:T(1,128)S(1)} fusion(f32[64,128,1]{1,2,0:T(1,128)S(1)} %bitcast.51, f32[64,128,128]{2,1,0:T(8,128)S(1)} %copy-done.1), kind=kOutput, calls=%fused_computation.88 | convolution fusion | flops 12582912 | bytes 4259840 | tf_op jit(solution)/shard_map/nrc,nc->nr/dot_general | solution.py:84
  133.0 0.3 fusion.20
  133.4 26.3 %psum.15 = f32[96,128]{1,0:T(8,128)S(1)} all-reduce(f32[96,128]{1,0:T(8,128)S(1)} %fusion.20), channel_id=1, replica_groups=mesh['grp'=8,'tm'=32] {'grp'}, use_global_device_ids=true, to_apply=%region_1.2 | all-reduce | flops 12288 | bytes 98304 | tf_op jit(solution)/shard_map/psum | solution.py:88
  159.7 1.9 %collective-permute-start.6 = (f32[32,128]{1,0:T(8,128)S(1)}, f32[32,128]{1,0:T(8,128)S(1)}, u32[]{:S(2)}, u32[]{:S(2)}) collective-permute-start(f32[32,128]{1,0:T(8,128)S(1)} %get-tuple-element.6), channel_id=1, source_target_pairs={{1,0},{2,1},{3,2},{4,3},{5,4},{6,5},{7,6},{8,7},{9,8},{10,9},{11,1... | collective-permute-start | bytes 49160 | tf_op jit(solution)/shard_map/ppermute | solution.py:29
  161.7 3.9 %collective-permute-start.7 = (f32[32,128]{1,0:T(8,128)S(1)}, f32[32,128]{1,0:T(8,128)S(1)}, u32[]{:S(2)}, u32[]{:S(2)}) collective-permute-start(f32[32,128]{1,0:T(8,128)S(1)} %get-tuple-element.7), channel_id=1, source_target_pairs={{0,1},{1,2},{2,3},{3,4},{4,5},{5,6},{6,7},{7,8},{8,9},{9,10},{10,1... | collective-permute-start | bytes 49160 | tf_op jit(solution)/shard_map/ppermute | solution.py:29
  165.6 9.8 %collective-permute-done.7 = f32[32,128]{1,0:T(8,128)S(1)} collective-permute-done((f32[32,128]{1,0:T(8,128)S(1)}, f32[32,128]{1,0:T(8,128)S(1)}, u32[]{:S(2)}, u32[]{:S(2)}) %collective-permute-start.7) | collective-permute-done | bytes 16416 | tf_op jit(solution)/shard_map/ppermute | solution.py:29
  175.4 0.6 add_multiply_fusion
  (22 shorter events, 0.1 us)
Async XLA Ops:
  0.6 25.7 %copy-start.5 = (f32[16,128]{1,0:T(8,128)S(1)}, f32[16,128]{1,0:T(8,128)}, u32[]{:S(2)}) copy-start(f32[16,128]{1,0:T(8,128)} %param.13) | copy-start | bytes 24580
  0.6 25.7 %copy-start.4 = (f32[16,128]{1,0:T(8,128)S(1)}, f32[16,128]{1,0:T(8,128)}, u32[]{:S(2)}) copy-start(f32[16,128]{1,0:T(8,128)} %param.11) | copy-start | bytes 24580
  0.7 13.7 %collective-permute-start.1 = (f32[32,128]{1,0:T(8,128)}, f32[32,128]{1,0:T(8,128)S(1)}, u32[]{:S(2)}, u32[]{:S(2)}) collective-permute-start(f32[32,128]{1,0:T(8,128)} %param.12), channel_id=1, source_target_pairs={{1,0},{2,1},{3,2},{4,3},{5,4},{6,5},{7,6},{8,7},{9,8},{10,9},{11,1... | collective-permute-start | bytes 49160 | tf_op jit(solution)/shard_map/ppermute | solution.py:21
  6.1 14.0 %collective-permute-start = (f32[32,128]{1,0:T(8,128)}, f32[32,128]{1,0:T(8,128)S(1)}, u32[]{:S(2)}, u32[]{:S(2)}) collective-permute-start(f32[32,128]{1,0:T(8,128)} %param.12), channel_id=1, source_target_pairs={{0,1},{1,2},{2,3},{3,4},{4,5},{5,6},{6,7},{7,8},{8,9},{9,10},{10,1... | collective-permute-start | bytes 49160 | tf_op jit(solution)/shard_map/ppermute | solution.py:18
  12.7 24.3 %copy-start = (f32[64,128,128]{2,1,0:T(8,128)S(1)}, f32[64,128,128]{2,1,0:T(8,128)}, u32[]{:S(2)}) copy-start(f32[64,128,128]{2,1,0:T(8,128)} %param.15) | copy-start | bytes 12582916
  21.0 73.0 %copy-start.2 = (f32[32,128]{1,0:T(8,128)S(1)}, f32[32,128]{1,0:T(8,128)}, u32[]{:S(2)}) copy-start(f32[32,128]{1,0:T(8,128)} %param.12) | copy-start | bytes 49156
  21.0 73.0 %copy-start.3 = (f32[32,128]{1,0:T(8,128)S(1)}, f32[32,128]{1,0:T(8,128)}, u32[]{:S(2)}) copy-start(f32[32,128]{1,0:T(8,128)} %param.14) | copy-start | bytes 49156
  72.7 53.7 %copy-start.1 = (f32[64,128,128]{2,1,0:T(8,128)S(1)}, f32[64,128,128]{2,1,0:T(8,128)}, u32[]{:S(2)}) copy-start(f32[64,128,128]{2,1,0:T(8,128)} %param.15) | copy-start | bytes 12582916
  72.8 9.4 %collective-permute-start.2 = (f32[32,128]{1,0:T(8,128)S(1)}, f32[32,128]{1,0:T(8,128)S(1)}, u32[]{:S(2)}, u32[]{:S(2)}) collective-permute-start(f32[32,128]{1,0:T(8,128)S(1)} %get-tuple-element.8), channel_id=1, source_target_pairs={{1,0},{2,1},{3,2},{4,3},{5,4},{6,5},{7,6},{8,7},{9,8},{10,9},{11,1... | collective-permute-start | bytes 49160 | tf_op jit(solution)/shard_map/ppermute | solution.py:29
  80.2 13.8 %collective-permute-start.3 = (f32[32,128]{1,0:T(8,128)S(1)}, f32[32,128]{1,0:T(8,128)S(1)}, u32[]{:S(2)}, u32[]{:S(2)}) collective-permute-start(f32[32,128]{1,0:T(8,128)S(1)} %get-tuple-element.9), channel_id=1, source_target_pairs={{0,1},{1,2},{2,3},{3,4},{4,5},{5,6},{6,7},{7,8},{8,9},{9,10},{10,1... | collective-permute-start | bytes 49160 | tf_op jit(solution)/shard_map/ppermute | solution.py:29
  94.0 6.0 %collective-permute-start.5 = (f32[32,128]{1,0:T(8,128)S(1)}, f32[32,128]{1,0:T(8,128)S(1)}, u32[]{:S(2)}, u32[]{:S(2)}) collective-permute-start(f32[32,128]{1,0:T(8,128)S(1)} %fusion.37), channel_id=1, source_target_pairs={{1,0},{2,1},{3,2},{4,3},{5,4},{6,5},{7,6},{8,7},{9,8},{10,9},{11,1... | collective-permute-start | bytes 49160 | tf_op jit(solution)/shard_map/ppermute | solution.py:21
  95.9 13.8 %collective-permute-start.4 = (f32[32,128]{1,0:T(8,128)S(1)}, f32[32,128]{1,0:T(8,128)S(1)}, u32[]{:S(2)}, u32[]{:S(2)}) collective-permute-start(f32[32,128]{1,0:T(8,128)S(1)} %fusion.37), channel_id=1, source_target_pairs={{0,1},{1,2},{2,3},{3,4},{4,5},{5,6},{6,7},{7,8},{8,9},{9,10},{10,1... | collective-permute-start | bytes 49160 | tf_op jit(solution)/shard_map/ppermute | solution.py:18
  126.2 49.8 %copy-start.6 = (f32[16,128]{1,0:T(8,128)}, f32[16,128]{1,0:T(8,128)S(1)}, u32[]{:S(2)}) copy-start(f32[16,128]{1,0:T(8,128)S(1)} %get-tuple-element.35) | copy-start | bytes 24580
  159.7 5.9 %collective-permute-start.6 = (f32[32,128]{1,0:T(8,128)S(1)}, f32[32,128]{1,0:T(8,128)S(1)}, u32[]{:S(2)}, u32[]{:S(2)}) collective-permute-start(f32[32,128]{1,0:T(8,128)S(1)} %get-tuple-element.6), channel_id=1, source_target_pairs={{1,0},{2,1},{3,2},{4,3},{5,4},{6,5},{7,6},{8,7},{9,8},{10,9},{11,1... | collective-permute-start | bytes 49160 | tf_op jit(solution)/shard_map/ppermute | solution.py:29
  161.7 13.8 %collective-permute-start.7 = (f32[32,128]{1,0:T(8,128)S(1)}, f32[32,128]{1,0:T(8,128)S(1)}, u32[]{:S(2)}, u32[]{:S(2)}) collective-permute-start(f32[32,128]{1,0:T(8,128)S(1)} %get-tuple-element.7), channel_id=1, source_target_pairs={{0,1},{1,2},{2,3},{3,4},{4,5},{5,6},{6,7},{7,8},{8,9},{9,10},{10,1... | collective-permute-start | bytes 49160 | tf_op jit(solution)/shard_map/ppermute | solution.py:29
where the time goes:
time: 177 us; the launch traced here: 176 us
  blocking collectives  55.2 us (31%)
  matrix products  47.4 us (27%)
  waiting for transfers between devices  37 us (21%)
  starting transfers between devices  28.6 us (16%)
  local copies, waits for them, and re-layouts  3.31 us (2%)
  other arithmetic  2.99 us (2%)
    psum x2, blocking collectives, body(): summed = lax.psum(window_terms, 'grp')  55.2 us
    ppermute x4, waiting for transfers between devices, shifted(): return lax.ppermute(block, axis, route)  21.6 us
    dot_general x2, matrix products, body(): jnp.dot(col_select.T, backward, precision=lax.Precision.HIGHEST)  21.5 us
    ppermute x2, waiting for transfers between devices, with_halo(): lax.ppermute(lax.slice_in_dim(block, block.shape[dim] - width, None, axis...  15.4 us
    ppermute x4, starting transfers between devices, shifted(): return lax.ppermute(block, axis, route)  15.2 us
    dot_general x2, matrix products, body(): jnp.einsum('nrc,nc->nr', tiles, primal_picked, precision=lax.Precision.HI...  13.2 us
    dot_general x2, matrix products, body(): jnp.einsum('nrc,nr->nc', tiles, dual_picked, precision=lax.Precision.HIGH...  10.6 us
    ppermute x2, starting transfers between devices, with_halo(): lax.ppermute(lax.slice_in_dim(block, 0, width, axis=dim), axis, backward)  7.35 us
  transfers between devices with their start and end apart: 8, of which 4 were waited for; matrix products, arithmetic and copies ran while one was open for 3% of the time, Pallas kernels for 0%

commit v1 on v0

v1 whole, which is shorter than its diff:
```python
import jax
import jax.numpy as jnp
from jax import lax
from jax.experimental import pallas as pl
from jax.experimental.pallas import tpu as pltpu
from jax.sharding import PartitionSpec as P

ITERS = 2
STEP = 0.6
MESH = pl.DeviceIdType.MESH
F32 = jnp.float32
BF16 = jnp.bfloat16

NT = 64
TILE = 128
CB = 16
RB = 32
OWN = 4
PIECE = RB // OWN
WIN = 3 * RB
CHUNK = 8

SLOTS = {0: (0, 24, 0), 1: (24, 16, 0), -1: (40, 16, 1), 2: (56, 8, 0), -2: (64, 8, 2)}
SLOT_ROWS = 72


def split(value):
    high = value.astype(BF16)
    return high, (value - high.astype(F32)).astype(BF16)


def kernel(
    x_ref,
    y_ref,
    cost_ref,
    rhs_ref,
    tiles_ref,
    rows_ref,
    cols_ref,
    count_ref,
    rowv_ref,
    class_ref,
    lower_ref,
    upper_ref,
    primal_out,
    dual_out,
    staged,
    weights,
    placed,
    product,
    picked,
    window_y,
    window_rhs,
    window_next,
    terms_a,
    terms_b,
    parts_a,
    parts_b,
    piece_a,
    piece_b,
    last_dual,
    load_sem,
    dual_sems,
    send_sems,
    recv_sems,
):
    group = lax.axis_index("grp")
    time = lax.axis_index("tm")
    place = group // 2
    core = lax.rem(group, 2)
    is_owner = core == 1

    def at(distance):
        return lax.rem(time + distance + 32, 32)

    def owner(offset):
        return lax.rem(place + offset, OWN)

    def far(distance):
        here, there = time // 16, at(distance) // 16
        return here != there

    loads = []
    for chunk in range(NT // CHUNK):
        span = pl.ds(chunk * CHUNK, CHUNK)
        load = pltpu.make_async_copy(tiles_ref.at[span], staged.at[span], load_sem.at[chunk])
        load.start()
        loads.append(load)

    barrier = pltpu.get_barrier_semaphore()

    def greet(target_group, target_time):
        pl.semaphore_signal(
            barrier, inc=1, device_id=(target_group, target_time), device_id_type=MESH
        )

    @pl.when(is_owner)
    def _():
        for distance in (2, -2, 1, -1, 0):
            for offset in (3, 2, 1, 0):
                if distance or offset:
                    greet(2 * owner(offset) + 1, at(distance))
                greet(2 * owner(offset), at(distance))
        at_end = (place == 0) | (place == 3)
        more = [jnp.where(far(distance), jnp.where(at_end, 2, 0), 1) for distance in (1, -1)]
        pl.semaphore_wait(barrier, 5 * OWN - 1 + OWN + more[0] + more[1])

    @pl.when(jnp.logical_not(is_owner))
    def _():
        for distance in (1, -1):
            source = jnp.where(far(distance), jnp.where(place >= 2, 0, 3), place)
            greet(2 * source + 1, at(distance))
        for offset in range(OWN):
            greet(2 * owner(offset) + 1, time)
        pl.semaphore_wait(barrier, 5 * OWN)

    def dual_copies(distance):
        slot = 1 - distance
        crossing = far(distance)
        at_end = (place == 0) | (place == 3)
        first = jnp.where(crossing, jnp.where(place == 3, 0, 2), place)
        second = lax.rem(first + 1, 4)

        def copy(target, number):
            return pltpu.make_async_remote_copy(
                src_ref=y_ref,
                dst_ref=window_y.at[:, slot],
                send_sem=dual_sems.at[slot // 2 * 4 + number],
                recv_sem=recv_sems.at[0],
                device_id=(target, at(distance)),
                device_id_type=MESH,
            )

        pairs = [
            (is_owner & (jnp.logical_not(crossing) | at_end), [copy(2 * first, 0), copy(2 * first + 1, 1)]),
            (is_owner & crossing & at_end, [copy(2 * second, 2), copy(2 * second + 1, 3)]),
        ]
        return pairs

    def rhs_copy(distance):
        slot = 1 - distance
        return pltpu.make_async_remote_copy(
            src_ref=rhs_ref.at[place],
            dst_ref=window_rhs.at[slot],
            send_sem=send_sems.at[1],
            recv_sem=recv_sems.at[1],
            device_id=(group, at(distance)),
            device_id_type=MESH,
        )

    for distance in (1, -1):
        for when, copies in dual_copies(distance):

            @pl.when(when)
            def _():
                for copy in copies:
                    copy.start()

    @pl.when(is_owner)
    def _():
        for distance in (1, -1):
            rhs_copy(distance).start()

    window_y[:, 1] = y_ref[...]
    window_rhs[1] = rhs_ref[place]

    for chunk in range(NT // CHUNK):
        loads[chunk].wait()

        def halve(slot, carry):
            high, low = split(staged[slot])
            base = pl.multiple_of(slot * TILE, TILE)
            weights[pl.ds(base, TILE), 0:TILE] = high
            weights[pl.ds(base, TILE), TILE : 2 * TILE] = low
            return carry

        lax.fori_loop(chunk * CHUNK, (chunk + 1) * CHUNK, halve, 0)

    var_class = class_ref[...]
    lower = jnp.zeros((CB, TILE), F32)
    upper = jnp.zeros((CB, TILE), F32)
    for class_id in range(lower_ref.shape[0]):
        lower = jnp.where(var_class == class_id, lower_ref[class_id], lower)
        upper = jnp.where(var_class == class_id, upper_ref[class_id], upper)

    count = count_ref[0]
    first_row = (time - 1) * RB
    first_col = (group * 32 + time) * CB
    window_id = lax.broadcasted_iota(jnp.int32, (WIN, NT), 0)
    owner_id = window_id // (3 * PIECE)
    block_id = window_id // PIECE - 3 * owner_id
    row_id = block_id * RB + owner_id * PIECE + lax.rem(window_id, PIECE)
    slot_id = lax.broadcasted_iota(jnp.int32, (WIN, NT), 1)
    scatter = ((rowv_ref[...] - first_row) == row_id) & (slot_id < count)
    scatter = jnp.where(scatter, 1.0, 0.0)
    scatter = jnp.concatenate([scatter, scatter], axis=1).astype(BF16)

    sub_id = lax.broadcasted_iota(jnp.int32, (CB, TILE), 0)

    def adjoint(field):
        for slot in range(NT):
            row = jnp.clip(rows_ref[slot] - first_row, 0, WIN - 1)
            block = row // RB
            inner = row - block * RB
            part = inner // PIECE
            value = field[part, block, pl.ds(inner - part * PIECE, 1), :]
            col = jnp.where(slot < count, cols_ref[slot] - first_col, -1)
            here = sub_id == col
            high = value.astype(BF16).astype(F32)
            low = value - high
            span = slice(slot * TILE, (slot + 1) * TILE)
            placed[0:CB, span] = jnp.where(here, high, 0.0).astype(BF16)
            placed[CB : 2 * CB, span] = jnp.where(here, low, 0.0).astype(BF16)
        total = jnp.dot(placed[...], weights[...], preferred_element_type=F32)
        total = total[:CB] + total[CB:]
        return total[:, :TILE] + total[:, TILE:]

    def forward(field):
        high, low = split(field)
        both = jnp.concatenate([high, low], axis=0)
        both = jnp.concatenate([both, both], axis=1)
        result = lax.dot_general(
            both, weights[...], (((1,), (1,)), ((), ())), preferred_element_type=F32
        )
        for slot in range(NT):
            span = slice(slot * TILE, (slot + 1) * TILE)
            product[slot] = result[:CB, span] + result[CB:, span]
        for slot in range(NT):
            col = jnp.clip(cols_ref[slot] - first_col, 0, CB - 1)
            picked[slot : slot + 1, :] = product[slot, pl.ds(col, 1), :]
        high, low = split(picked[...])
        return jnp.dot(scatter, jnp.concatenate([high, low], axis=0), preferred_element_type=F32)

    def primal_update(primal, adjoint_part):
        moved = primal - STEP * (cost_ref[...] - adjoint_part)
        return jnp.minimum(jnp.maximum(moved, lower), upper)

    def to_owner(source, target, distance, offset, sems):
        return pltpu.make_async_remote_copy(
            src_ref=source,
            dst_ref=target,
            send_sem=send_sems.at[sems],
            recv_sem=recv_sems.at[sems],
            device_id=(2 * owner(offset) + 1, at(distance)),
            device_id_type=MESH,
        )

    def from_owner(source, target, offset, sems):
        return pltpu.make_async_remote_copy(
            src_ref=source,
            dst_ref=target,
            send_sem=send_sems.at[sems],
            recv_sem=recv_sems.at[sems],
            device_id=(lax.rem(group + offset, 8), time),
            device_id_type=MESH,
        )

    def spans_a(distance, offset):
        first, rows, block = SLOTS[-distance]
        source = terms_a.at[pl.ds(pl.multiple_of(owner(offset) * 3 * PIECE + block * PIECE, 8), rows)]
        return source, parts_a.at[pl.ds(pl.multiple_of(group * SLOT_ROWS + first, 8), rows)]

    def spans_b(distance, offset):
        source = terms_b.at[pl.ds(pl.multiple_of(owner(offset) * 3 * PIECE + (1 + distance) * PIECE, 8), PIECE)]
        return source, parts_b.at[pl.ds(pl.multiple_of(group * 3 * PIECE + (1 - distance) * PIECE, 8), PIECE)]

    def scatter_sum(distances, spans, sems):
        for distance in distances:
            for offset in (3, 2, 1, 0):
                source, target = spans(distance, offset)
                if distance or offset:
                    to_owner(source, target, distance, offset, sems).start()
                else:

                    @pl.when(jnp.logical_not(is_owner))
                    def _():
                        to_owner(source, target, distance, offset, sems).start()

    def wait_recv(ref, sems):
        pltpu.make_async_copy(ref, ref, recv_sems.at[sems]).wait()

    def wait_send(ref, sems):
        pltpu.make_async_copy(ref, ref, send_sems.at[sems]).wait()

    wait_recv(window_y.at[:, 0:2], 0)
    primal_0 = x_ref[...]
    primal_1 = primal_update(primal_0, adjoint(window_y))
    terms_a[...] = forward(2.0 * primal_1 - primal_0)
    scatter_sum((2, -2, 1, -1, 0), spans_a, 2)

    @pl.when(is_owner)
    def _():
        own = pl.ds(pl.multiple_of(place * 3 * PIECE, 8), 3 * PIECE)
        parts_a[pl.ds(pl.multiple_of(group * SLOT_ROWS, 8), 3 * PIECE)] = terms_a[own]
        wait_recv(window_rhs.at[0:2], 1)
        wait_recv(parts_a.at[0 : 8 * SLOT_ROWS - 3 * PIECE], 2)
        sums = jnp.sum(parts_a[...].reshape(8, SLOT_ROWS, TILE), axis=0)
        image = jnp.concatenate(
            [
                sums[0:8] + sums[40:48] + sums[64:72],
                sums[8:16] + sums[24:32] + sums[48:56],
                sums[16:24] + sums[32:40] + sums[56:64],
            ],
            axis=0,
        )
        for block in range(3):
            span = slice(block * PIECE, (block + 1) * PIECE)
            piece_a[block] = jnp.maximum(
                window_y[place, block] + STEP * (window_rhs[block] - image[span]), 0.0
            )
        for offset in range(7, 0, -1):
            from_owner(piece_a, window_next.at[place], offset, 3).start()
        window_next[place] = piece_a[...]
        wait_recv(window_next.at[0:3], 3)

    @pl.when(jnp.logical_not(is_owner))
    def _():
        wait_recv(window_next, 3)

    primal_2 = primal_update(primal_1, adjoint(window_next))
    terms_b[...] = forward(2.0 * primal_2 - primal_1)
    scatter_sum((1, -1, 0), spans_b, 4)
    primal_out[0] = primal_1
    primal_out[1] = primal_2
    dual_out[0] = window_next[:, 1]

    @pl.when(is_owner)
    def _():
        own = pl.ds(pl.multiple_of(place * 3 * PIECE + PIECE, 8), PIECE)
        parts_b[pl.ds(pl.multiple_of(group * 3 * PIECE + PIECE, 8), PIECE)] = terms_b[own]
        wait_recv(parts_b.at[0 : 23 * PIECE], 4)
        sums = jnp.sum(parts_b[...].reshape(8, 3 * PIECE, TILE), axis=0)
        image = sums[0:8] + sums[8:16] + sums[16:24]
        piece_b[...] = jnp.maximum(piece_a[1] + STEP * (window_rhs[1] - image), 0.0)
        for offset in range(7, 0, -1):
            from_owner(piece_b, last_dual.at[place], offset, 5).start()
        last_dual[place] = piece_b[...]
        wait_recv(last_dual.at[0:3], 5)

    @pl.when(jnp.logical_not(is_owner))
    def _():
        wait_recv(last_dual, 5)

    dual_out[1] = last_dual[...]

    for distance in (1, -1):
        for when, copies in dual_copies(distance):

            @pl.when(when)
            def _():
                for copy in copies:
                    copy.wait_send()

    @pl.when(is_owner)
    def _():
        wait_send(window_rhs.at[0:2], 1)
        wait_send(parts_a.at[0 : 33 * PIECE], 2)
        wait_send(parts_a.at[0 : 21 * PIECE], 3)
        wait_send(parts_a.at[0 : 11 * PIECE], 4)
        wait_send(parts_a.at[0 : 7 * PIECE], 5)

    @pl.when(jnp.logical_not(is_owner))
    def _():
        wait_send(parts_a.at[0 : 36 * PIECE], 2)
        wait_send(parts_a.at[0 : 12 * PIECE], 4)


def means(primals_ref, duals_ref, primal_out, dual_out, primal_mean_out, dual_mean_out):
    for iterates, last, mean in ((primals_ref, primal_out, primal_mean_out), (duals_ref, dual_out, dual_mean_out)):
        last[...] = iterates[1]
        mean[...] = (iterates[0] + iterates[1]) / ITERS


def body(
    x_start,
    y_start,
    cost,
    rhs,
    tiles,
    tile_rows,
    tile_cols,
    tile_count,
    var_class,
    lower_table,
    upper_table,
):
    vmem = pl.BlockSpec(memory_space=pltpu.VMEM)
    smem = pl.BlockSpec(memory_space=pltpu.SMEM)
    primals, duals = pl.pallas_call(
        kernel,
        name="pdhg",
        out_shape=(
            jax.ShapeDtypeStruct((ITERS, CB, TILE), F32),
            jax.ShapeDtypeStruct((ITERS, OWN, PIECE, TILE), F32),
        ),
        in_specs=[vmem, vmem, vmem, vmem, pl.BlockSpec(memory_space=pl.ANY), smem, smem, smem, vmem, vmem, smem, smem],
        out_specs=(vmem, vmem),
        scratch_shapes=[
            pltpu.VMEM((NT, TILE, TILE), F32),
            pltpu.VMEM((NT * TILE, 2 * TILE), BF16),
            pltpu.VMEM((2 * CB, NT * TILE), BF16),
            pltpu.VMEM((NT, CB, TILE), F32),
            pltpu.VMEM((NT, TILE), F32),
            pltpu.VMEM((OWN, 3, PIECE, TILE), F32),
            pltpu.VMEM((3, PIECE, TILE), F32),
            pltpu.VMEM((OWN, 3, PIECE, TILE), F32),
            pltpu.VMEM((WIN, TILE), F32),
            pltpu.VMEM((WIN, TILE), F32),
            pltpu.VMEM((8 * SLOT_ROWS, TILE), F32),
            pltpu.VMEM((8 * 3 * PIECE, TILE), F32),
            pltpu.VMEM((3, PIECE, TILE), F32),
            pltpu.VMEM((PIECE, TILE), F32),
            pltpu.VMEM((OWN, PIECE, TILE), F32),
            pltpu.SemaphoreType.DMA((NT // CHUNK,)),
            pltpu.SemaphoreType.DMA((8,)),
            pltpu.SemaphoreType.DMA((6,)),
            pltpu.SemaphoreType.DMA((6,)),
        ],
        compiler_params=pltpu.CompilerParams(
            collective_id=0, has_side_effects=True, vmem_limit_bytes=60 * 1024 * 1024
        ),
    )(
        x_start,
        y_start.reshape(OWN, PIECE, TILE),
        cost,
        rhs.reshape(OWN, PIECE, TILE),
        tiles,
        tile_rows,
        tile_cols,
        tile_count,
        tile_rows.reshape(1, NT),
        var_class,
        lower_table,
        upper_table,
    )
    columns = jax.ShapeDtypeStruct((CB, TILE), F32)
    rows = jax.ShapeDtypeStruct((RB, TILE), F32)
    return pl.pallas_call(
        means,
        name="means",
        out_shape=(columns, rows, columns, rows),
        in_specs=[vmem, vmem],
        out_specs=(vmem, vmem, vmem, vmem),
    )(primals, duals.reshape(ITERS, RB, TILE))


def solution(mesh):
    return jax.shard_map(
        body,
        mesh=mesh,
        in_specs=(
            P(("grp", "tm"), None),
            P("tm", None),
            P(("grp", "tm"), None),
            P("tm", None),
            P(("grp", "tm"), None, None),
            P(("grp", "tm")),
            P(("grp", "tm")),
            P(("grp", "tm")),
            P(("grp", "tm"), None),
            P(),
            P(),
        ),
        out_specs=(P(("grp", "tm"), None), P("tm", None), P(("grp", "tm"), None), P("tm", None)),
        check_vma=False,
    )
```

time: 177 us -> 47.4 us (0.27)
  the two profiles are of different devices: /device:TPU:128 before, /device:TPU:1 now
where the time goes in v1:
time: 47.4 us; the launch traced here: 47.1 us
  Pallas kernels  45.8 us (97%)
  between operations  1.29 us (3%)
    pallas_call x1, Pallas kernels, body(): pl.pallas_call(kernel, name='pdhg', out_shape=(jax.ShapeDtypeStruct((ITER...  44.4 us
    pallas_call x1, Pallas kernels, body(): pl.pallas_call(means, name='means', out_shape=(columns, rows, columns, ro...  1.4 us

profile of v1, /device:TPU:1, one launch (start us, length us, event | category | flops | bytes accessed | tf_op | source)
XLA Modules:
  0.0 47.1 jit_solution(12895081885476375914)
XLA Ops:
  1.3 44.4 %pdhg.1 = (f32[2,16,128]{2,1,0:T(8,128)}, f32[2,4,8,128]{3,2,1,0:T(8,128)}) custom-call(f32[16,128]{1,0:T(8,128)} %x_ref.1, f32[4,8,128]{2,1,0:T(8,128)} %bitcast.5, f32[16,128]{1,0:T(8,128)} %cost_ref.1, f32[4,8,128]{2,1,0:T(8,128)} %bitcast.6, f32[64,128,128]{2,1,0:T(8,128)} %tiles_ref.1, s32[64]{0:T(128)} %rows_ref.1, s32[64]{0:T(128)} %cols_ref.1, ...), custom_call_target="tpu_custom_call" | custom-call | tf_op jit(solution)/shard_map/pdhg/pallas_call | solution.py:389
  45.7 1.4 %means.1 = (f32[16,128]{1,0:T(8,128)}, f32[32,128]{1,0:T(8,128)}, f32[16,128]{1,0:T(8,128)}, f32[32,128]{1,0:T(8,128)}) custom-call(f32[2,16,128]{2,1,0:T(8,128)} %get-tuple-element.6.primals_ref, f32[2,32,128]{2,1,0:T(8,128)} %bitcast.4), custom_call_target="tpu_custom_call" | custom-call | tf_op jit(solution)/shard_map/means/pallas_call | solution.py:438

commit v2 on v1

v2 whole, which is shorter than its diff:
```python
import jax
import jax.numpy as jnp
from jax import lax
from jax.experimental import pallas as pl
from jax.experimental.pallas import tpu as pltpu
from jax.sharding import PartitionSpec as P

ITERS = 2
STEP = 0.6
MESH = pl.DeviceIdType.MESH
F32 = jnp.float32
BF16 = jnp.bfloat16

NT = 64
TILE = 128
CB = 16
RB = 32
OWN = 4
PIECE = RB // OWN
WIN = 3 * RB
CHUNK = 8

LAST, NEXT = 15, 16
SLOT_ROWS = 6 * PIECE


def split(value):
    high = value.astype(BF16)
    return high, (value - high.astype(F32)).astype(BF16)


def kernel(
    x_hbm,
    y_hbm,
    cost_hbm,
    rhs_hbm,
    tiles_hbm,
    cols_hbm,
    count_hbm,
    rowv_hbm,
    colv_hbm,
    class_hbm,
    lower_hbm,
    upper_hbm,
    primal_out,
    dual_out,
    x_ref,
    y_ref,
    cost_ref,
    rhs_ref,
    cols_ref,
    count_ref,
    rowv_ref,
    colv_ref,
    class_ref,
    lower_ref,
    upper_ref,
    staged,
    turned,
    factors,
    select,
    partial,
    pick,
    window_y,
    window_rhs,
    window_next,
    terms_a,
    terms_b,
    parts_a,
    parts_b,
    piece_a,
    piece_b,
    last_dual,
    load_sem,
    input_sems,
    dual_sems,
    halo_sems,
    sums_sent,
    sums_recv,
    send_sems,
    recv_sems,
):
    group = lax.axis_index("grp")
    time = lax.axis_index("tm")
    place = group // 2
    core = lax.rem(group, 2)
    is_owner = core == 1

    def at(distance):
        return time + distance

    def exists(distance):
        there = time + distance
        return (there >= 0) & (there < 32)

    def number(distances):
        return sum(jnp.where(exists(distance), 1, 0) for distance in distances)

    def owner(offset):
        return lax.rem(place + offset, OWN)

    def far(distance):
        return (time == LAST) if distance > 0 else (time == NEXT)

    def near(distance):
        return exists(distance) & jnp.logical_not(far(distance))

    edge = (time == LAST) | (time == NEXT)
    at_end = (place == 0) | (place == 3)

    def both(distance):
        return edge if distance == 0 else far(distance)

    parts_a[...] = jnp.zeros_like(parts_a)
    parts_b[...] = jnp.zeros_like(parts_b)
    window_y[...] = jnp.zeros_like(window_y)
    window_next[...] = jnp.zeros_like(window_next)
    window_rhs[...] = jnp.zeros_like(window_rhs)

    barrier = pltpu.get_barrier_semaphore()

    def greet(target_group, target_time):
        pl.semaphore_signal(
            barrier, inc=1, device_id=(target_group, target_time), device_id_type=MESH
        )

    def greet_all(distance):
        for offset in (3, 2, 1, 0):
            if distance or offset:
                greet(2 * owner(offset) + 1, at(distance))
            greet(2 * owner(offset), at(distance))

    @pl.when(is_owner)
    def _():
        for distance, when in ((2, time == LAST), (-2, time == NEXT), (1, exists(1)), (-1, exists(-1))):

            @pl.when(when)
            def _():
                greet_all(distance)

        greet_all(0)

    @pl.when(jnp.logical_not(is_owner))
    def _():
        for distance in (1, -1):

            @pl.when(far(distance))
            def _():
                greet(2 * jnp.where(place >= 2, 0, 3) + 1, at(distance))

            @pl.when(near(distance))
            def _():
                for offset in range(OWN):
                    greet(2 * owner(offset) + 1, at(distance))

        for offset in range(OWN):
            greet(2 * owner(offset) + 1, time)

    inputs = []
    for index, (source, target) in enumerate(
        (
            (y_hbm, y_ref),
            (rhs_hbm, rhs_ref),
            (x_hbm, x_ref),
            (cost_hbm, cost_ref),
            (class_hbm, class_ref),
            (rowv_hbm, rowv_ref),
            (colv_hbm, colv_ref),
            (count_hbm, count_ref),
            (lower_hbm, lower_ref),
            (upper_hbm, upper_ref),
            (cols_hbm, cols_ref),
        )
    ):
        copy = pltpu.make_async_copy(source, target, input_sems.at[index])
        copy.start()
        inputs.append(copy)
    loads = []
    for chunk in range(NT // CHUNK):
        span = pl.ds(chunk * CHUNK, CHUNK)
        load = pltpu.make_async_copy(tiles_hbm.at[span], staged.at[span], load_sem.at[chunk])
        load.start()
        loads.append(load)
    for copy in inputs:
        copy.wait()

    of_owner = 7
    for distance in (1, -1):
        of_owner = of_owner + jnp.where(near(distance), 8, 0)
        of_owner = of_owner + jnp.where(far(distance), jnp.where(at_end, 6, 4), 0)
    two_steps = jnp.where((time == LAST - 1) | (time == NEXT + 1), OWN, 0)
    of_other = OWN * number((1, 0, -1))
    pl.semaphore_wait(barrier, jnp.where(is_owner, of_owner, of_other) + two_steps)

    def dual_copies(distance):
        slot = 1 - distance
        crossing = far(distance)
        first = jnp.where(crossing, jnp.where(place == 3, 0, 2), place)
        second = lax.rem(first + 1, 4)

        def copy(target, number):
            return pltpu.make_async_remote_copy(
                src_ref=y_ref,
                dst_ref=window_y.at[:, slot],
                send_sem=dual_sems.at[slot // 2 * 4 + number],
                recv_sem=halo_sems.at[slot],
                device_id=(target, at(distance)),
                device_id_type=MESH,
            )

        pairs = [
            (is_owner & exists(distance) & (jnp.logical_not(crossing) | at_end), [copy(2 * first, 0), copy(2 * first + 1, 1)]),
            (is_owner & crossing & at_end, [copy(2 * second, 2), copy(2 * second + 1, 3)]),
        ]
        return pairs

    def rhs_copy(distance):
        slot = 1 - distance
        return pltpu.make_async_remote_copy(
            src_ref=rhs_ref.at[place],
            dst_ref=window_rhs.at[slot],
            send_sem=halo_sems.at[slot + 4],
            recv_sem=halo_sems.at[slot + 1],
            device_id=(group, at(distance)),
            device_id_type=MESH,
        )

    for distance in (1, -1):
        for when, copies in dual_copies(distance):

            @pl.when(when)
            def _():
                for copy in copies:
                    copy.start()

    @pl.when(is_owner)
    def _():
        for distance in (1, -1):

            @pl.when(far(distance))
            def _():
                rhs_copy(distance).start()

    window_y[:, 1] = y_ref[...]
    window_rhs[1] = rhs_ref[place]

    for chunk in range(NT // CHUNK):
        loads[chunk].wait()

        def turn(slot, carry):
            turned[slot] = staged[slot].T
            return carry

        lax.fori_loop(chunk * CHUNK, (chunk + 1) * CHUNK, turn, 0, unroll=4)

    var_class = class_ref[...]
    lower = jnp.zeros((CB, TILE), F32)
    upper = jnp.zeros((CB, TILE), F32)
    for class_id in range(lower_ref.shape[1]):
        lower = jnp.where(var_class == class_id, lower_ref[:, class_id : class_id + 1], lower)
        upper = jnp.where(var_class == class_id, upper_ref[:, class_id : class_id + 1], upper)

    first_row = (time - 1) * RB
    first_col = (group * 32 + time) * CB
    slot_id = lax.broadcasted_iota(jnp.int32, (WIN, NT), 1)
    window_id = lax.broadcasted_iota(jnp.int32, (WIN, NT), 0)
    owner_id = window_id // (3 * PIECE)
    block_id = window_id // PIECE - 3 * owner_id
    row_id = block_id * RB + owner_id * PIECE + lax.rem(window_id, PIECE)
    scatter = ((rowv_ref[...] - first_row) == row_id) & (slot_id < count_ref[0])
    gather = ((colv_ref[...] - first_col) == window_id[:CB]) & (slot_id[:CB] < count_ref[0])
    scatter = jnp.where(scatter, 1.0, 0.0)
    chosen = jnp.concatenate([scatter, jnp.where(gather, 1.0, 0.0)], axis=0)
    pick[...] = jnp.concatenate([scatter, scatter], axis=0).astype(BF16)
    spread = lax.broadcasted_iota(jnp.int32, (NT, 8 * NT), 1) // 8 == lax.broadcasted_iota(jnp.int32, (NT, 8 * NT), 0)
    chosen = jnp.dot(chosen.astype(BF16), jnp.where(spread, 1.0, 0.0).astype(BF16), preferred_element_type=F32)
    chosen = chosen.astype(BF16)
    select[...] = jnp.concatenate([chosen, chosen], axis=1)

    def add_up(first, last):
        high, low = split(partial[...])
        return jnp.dot(
            select[first:last], jnp.concatenate([high, low], axis=0), preferred_element_type=F32
        )

    def fold(value):
        return jnp.sum(value.reshape(TILE // 8, 8, TILE), axis=0)

    def adjoint(field):
        high, low = split(field[...].reshape(WIN, TILE).T)
        columns = jnp.dot(
            jnp.concatenate([high, low], axis=1), pick[...], preferred_element_type=F32
        )
        for slot in range(NT):
            factor = jnp.broadcast_to(columns[:, slot : slot + 1], (TILE, TILE))
            partial[8 * slot : 8 * slot + 8] = fold(staged[slot] * factor)
        return add_up(WIN, WIN + CB)

    def forward(field):
        columns = field.T
        for block in range(CB):
            factors[block] = jnp.broadcast_to(columns[:, block : block + 1], (TILE, TILE))
        for slot in range(NT):
            col = jnp.clip(cols_ref[slot] - first_col, 0, CB - 1)
            partial[8 * slot : 8 * slot + 8] = fold(turned[slot] * factors[col])
        return add_up(0, WIN)

    def primal_update(primal, adjoint_part):
        moved = primal - STEP * (cost_ref[...] - adjoint_part)
        return jnp.minimum(jnp.maximum(moved, lower), upper)

    def to_owner(source, target, distance, offset, sems):
        return pltpu.make_async_remote_copy(
            src_ref=source,
            dst_ref=target,
            send_sem=sums_sent.at[sems, distance + 2],
            recv_sem=sums_recv.at[sems, 2 - distance],
            device_id=(2 * owner(offset) + 1, at(distance)),
            device_id_type=MESH,
        )

    def from_owner(source, target, offset, distance, semaphore):
        return pltpu.make_async_remote_copy(
            src_ref=source,
            dst_ref=target,
            send_sem=send_sems.at[semaphore],
            recv_sem=recv_sems.at[semaphore],
            device_id=(lax.rem(group + offset, 8), at(distance)),
            device_id_type=MESH,
        )

    def rows_of(ref, first, pieces):
        return ref.at[pl.ds(pl.multiple_of(first, PIECE), pieces * PIECE)]

    def copy_a(distance, offset, pieces):
        block = jnp.where(time == NEXT, 0, 1) if distance == 0 else 2 if distance > 0 else 0
        if pieces == 2:
            block = jnp.where(time == NEXT, 0, 1)
        region = {
            0: 0,
            1: jnp.where(time + 1 == NEXT, 2, 4),
            -1: jnp.where(time - 1 == NEXT, 4, 2),
            2: 5,
            -2: 5,
        }[distance]
        if distance == 0 and pieces == 1:
            block = 1
        source = rows_of(terms_a, (owner(offset) * 3 + block) * PIECE, pieces)
        target = rows_of(parts_a, group * SLOT_ROWS + region * PIECE, pieces)
        return to_owner(source, target, distance, offset, 0)

    def copy_b(distance, offset):
        source = rows_of(terms_b, (owner(offset) * 3 + 1 + distance) * PIECE, 1)
        target = rows_of(parts_b, (group * 3 + 1 - distance) * PIECE, 1)
        return to_owner(source, target, distance, offset, 1)

    def to_owners(distance, copy):
        for offset in (3, 2, 1, 0):
            if distance or offset:
                copy(distance, offset).start()
            else:

                @pl.when(jnp.logical_not(is_owner))
                def _():
                    copy(distance, offset).start()

    def steps_a():
        for distance in (1, -1, 0):
            yield distance, exists(distance) & both(distance), 2
        for distance in (1, -1, 0):
            yield distance, exists(distance) & jnp.logical_not(both(distance)), 1

    def wait_rows(semaphore, pieces):
        ref = parts_a.at[0 : pieces * PIECE]
        pltpu.make_async_copy(ref, ref, semaphore).wait()

    def wait_sums_a(semaphores, two_steps, copies, own):
        for distance, when, pieces in steps_a():

            @pl.when(when)
            def _():
                wait_rows(semaphores.at[0, distance + 2], pieces * (copies if distance else own))

        for distance, when in two_steps:

            @pl.when(when)
            def _():
                wait_rows(semaphores.at[0, distance + 2], copies)

    def wait_sums_b(semaphores, copies, own):
        for distance in (1, -1, 0):

            @pl.when(exists(distance))
            def _():
                wait_rows(semaphores.at[1, distance + 2], copies if distance else own)

    for distance in (1, -1):

        @pl.when(exists(distance))
        def _():
            dual_in = window_y.at[:, 1 + distance]
            pltpu.make_async_copy(dual_in, dual_in, halo_sems.at[1 + distance]).wait()

    primal_0 = x_ref[...]
    primal_1 = primal_update(primal_0, adjoint(window_y))
    terms_a[...] = forward(2.0 * primal_1 - primal_0)
    for distance, when in ((2, time == LAST - 1), (-2, time == NEXT + 1)):

        @pl.when(when)
        def _():
            to_owners(distance, lambda distance, offset: copy_a(distance, offset, 1))

    for distance, when, pieces in steps_a():

        @pl.when(when)
        def _():
            to_owners(distance, lambda distance, offset: copy_a(distance, offset, pieces))

    @pl.when(is_owner)
    def _():
        for pieces, when in ((2, edge), (1, jnp.logical_not(edge))):

            @pl.when(when)
            def _():
                block = jnp.where(time == NEXT, 0, 1) if pieces == 2 else 1
                source = pl.ds(pl.multiple_of((place * 3 + block) * PIECE, 8), pieces * PIECE)
                target = pl.ds(pl.multiple_of(group * SLOT_ROWS, 8), pieces * PIECE)
                parts_a[target] = terms_a[source]

        for distance in (1, -1):

            @pl.when(far(distance))
            def _():
                rhs_in = window_rhs.at[1 + distance]
                pltpu.make_async_copy(rhs_in, rhs_in, halo_sems.at[2 + distance]).wait()

        wait_sums_a(sums_recv, ((2, time == LAST), (-2, time == NEXT)), 8, 7)
        sums = jnp.sum(parts_a[...].reshape(8, SLOT_ROWS, TILE), axis=0)
        low = sums[0:8] + sums[16:24]
        high = sums[8:16] + sums[24:32]
        upper_side = time == NEXT
        first = jnp.where(upper_side, high, low) + sums[32:40]
        second = jnp.where(upper_side, low, high) + sums[40:48]
        for block in range(3):
            image = first if block == 1 else second
            piece_a[block] = jnp.maximum(window_y[place, block] + STEP * (window_rhs[block] - image), 0.0)
        for distance in (1, -1):

            @pl.when(near(distance))
            def _():
                for offset in range(7, -1, -1):
                    from_owner(
                        piece_a.at[1], window_next.at[place, 1 - distance], offset, distance, 2 + distance
                    ).start()

        @pl.when(edge)
        def _():
            span = pl.ds(jnp.where(time == NEXT, 0, 1), 2)
            for offset in range(7, 0, -1):
                from_owner(piece_a.at[span], window_next.at[place, span], offset, 0, 0).start()
            window_next[place, span] = piece_a[span]

        @pl.when(jnp.logical_not(edge))
        def _():
            for offset in range(7, 0, -1):
                from_owner(piece_a.at[1], window_next.at[place, 1], offset, 0, 0).start()
            window_next[place, 1] = piece_a[1]

    for owned, others in ((is_owner, OWN - 1), (jnp.logical_not(is_owner), OWN)):
        for pieces, when in ((2, edge), (1, jnp.logical_not(edge))):

            @pl.when(owned & when)
            def _():
                wait_rows(recv_sems.at[0], pieces * others)

    for distance in (1, -1):

        @pl.when(near(distance))
        def _():
            wait_rows(recv_sems.at[2 - distance], OWN)

    primal_2 = primal_update(primal_1, adjoint(window_next))
    terms_b[...] = forward(2.0 * primal_2 - primal_1)
    for distance in (1, -1, 0):

        @pl.when(exists(distance))
        def _():
            to_owners(distance, copy_b)

    primal_out[0] = primal_1
    primal_out[1] = primal_2
    dual_out[0] = window_next[:, 1]

    @pl.when(is_owner)
    def _():
        own = pl.ds(pl.multiple_of(place * 3 * PIECE + PIECE, 8), PIECE)
        parts_b[pl.ds(pl.multiple_of(group * 3 * PIECE + PIECE, 8), PIECE)] = terms_b[own]
        wait_sums_b(sums_recv, 8, 7)
        sums = jnp.sum(parts_b[...].reshape(8, 3 * PIECE, TILE), axis=0)
        image = sums[0:8] + sums[8:16] + sums[16:24]
        piece_b[...] = jnp.maximum(piece_a[1] + STEP * (window_rhs[1] - image), 0.0)
        for offset in range(7, 0, -1):
            from_owner(piece_b, last_dual.at[place], offset, 0, 2).start()
        last_dual[place] = piece_b[...]
        wait_rows(recv_sems.at[2], OWN - 1)

    @pl.when(jnp.logical_not(is_owner))
    def _():
        wait_rows(recv_sems.at[2], OWN)

    dual_out[1] = last_dual[...]

    for distance in (1, -1):
        for when, copies in dual_copies(distance):

            @pl.when(when)
            def _():
                for copy in copies:
                    copy.wait_send()

    two_steps = ((2, time == LAST - 1), (-2, time == NEXT + 1))

    @pl.when(is_owner)
    def _():
        for distance in (1, -1):

            @pl.when(far(distance))
            def _():
                rhs_copy(distance).wait_send()

            @pl.when(near(distance))
            def _():
                wait_rows(send_sems.at[2 + distance], 8)

        wait_sums_a(sums_sent, two_steps, OWN, OWN - 1)
        wait_sums_b(sums_sent, OWN, OWN - 1)
        for pieces, when in ((2, edge), (1, jnp.logical_not(edge))):

            @pl.when(when)
            def _():
                wait_rows(send_sems.at[0], 7 * pieces)

        wait_rows(send_sems.at[2], 7)

    @pl.when(jnp.logical_not(is_owner))
    def _():
        wait_sums_a(sums_sent, two_steps, OWN, OWN)
        wait_sums_b(sums_sent, OWN, OWN)


def means(primals_ref, duals_ref, primal_out, dual_out, primal_mean_out, dual_mean_out):
    for iterates, last, mean in ((primals_ref, primal_out, primal_mean_out), (duals_ref, dual_out, dual_mean_out)):
        last[...] = iterates[1]
        mean[...] = (iterates[0] + iterates[1]) / ITERS


def body(
    x_start,
    y_start,
    cost,
    rhs,
    tiles,
    tile_rows,
    tile_cols,
    tile_count,
    var_class,
    lower_table,
    upper_table,
):
    vmem = pl.BlockSpec(memory_space=pltpu.VMEM)
    primals, duals = pl.pallas_call(
        kernel,
        name="pdhg",
        out_shape=(
            jax.ShapeDtypeStruct((ITERS, CB, TILE), F32),
            jax.ShapeDtypeStruct((ITERS, OWN, PIECE, TILE), F32),
        ),
        in_specs=[pl.BlockSpec(memory_space=pltpu.HBM)] * 12,
        out_specs=(vmem, vmem),
        scratch_shapes=[
            pltpu.VMEM((CB, TILE), F32),
            pltpu.VMEM((OWN, PIECE, TILE), F32),
            pltpu.VMEM((CB, TILE), F32),
            pltpu.VMEM((OWN, PIECE, TILE), F32),
            pltpu.SMEM((NT,), jnp.int32),
            pltpu.SMEM((1,), jnp.int32),
            pltpu.VMEM((1, NT), jnp.int32),
            pltpu.VMEM((1, NT), jnp.int32),
            pltpu.VMEM((CB, TILE), jnp.int32),
            pltpu.VMEM((1, 8), F32),
            pltpu.VMEM((1, 8), F32),
            pltpu.VMEM((NT, TILE, TILE), F32),
            pltpu.VMEM((NT, TILE, TILE), F32),
            pltpu.VMEM((CB, TILE, TILE), F32),
            pltpu.VMEM((WIN + CB, 16 * NT), BF16),
            pltpu.VMEM((8 * NT, TILE), F32),
            pltpu.VMEM((2 * WIN, NT), BF16),
            pltpu.VMEM((OWN, 3, PIECE, TILE), F32),
            pltpu.VMEM((3, PIECE, TILE), F32),
            pltpu.VMEM((OWN, 3, PIECE, TILE), F32),
            pltpu.VMEM((WIN, TILE), F32),
            pltpu.VMEM((WIN, TILE), F32),
            pltpu.VMEM((8 * SLOT_ROWS, TILE), F32),
            pltpu.VMEM((8 * 3 * PIECE, TILE), F32),
            pltpu.VMEM((3, PIECE, TILE), F32),
            pltpu.VMEM((PIECE, TILE), F32),
            pltpu.VMEM((OWN, PIECE, TILE), F32),
            pltpu.SemaphoreType.DMA((NT // CHUNK,)),
            pltpu.SemaphoreType.DMA((11,)),
            pltpu.SemaphoreType.DMA((8,)),
            pltpu.SemaphoreType.DMA((8,)),
            pltpu.SemaphoreType.DMA((2, 5)),
            pltpu.SemaphoreType.DMA((2, 5)),
            pltpu.SemaphoreType.DMA((4,)),
            pltpu.SemaphoreType.DMA((4,)),
        ],
        compiler_params=pltpu.CompilerParams(
            collective_id=0, has_side_effects=True, vmem_limit_bytes=60 * 1024 * 1024
        ),
    )(
        x_start,
        y_start.reshape(OWN, PIECE, TILE),
        cost,
        rhs.reshape(OWN, PIECE, TILE),
        tiles,
        tile_cols,
        tile_count,
        tile_rows.reshape(1, NT),
        tile_cols.reshape(1, NT),
        var_class,
        lower_table.reshape(1, 8),
        upper_table.reshape(1, 8),
    )
    columns = jax.ShapeDtypeStruct((CB, TILE), F32)
    rows = jax.ShapeDtypeStruct((RB, TILE), F32)
    return pl.pallas_call(
        means,
        name="means",
        out_shape=(columns, rows, columns, rows),
        in_specs=[vmem, vmem],
        out_specs=(vmem, vmem, vmem, vmem),
    )(primals, duals.reshape(ITERS, RB, TILE))


def solution(mesh):
    return jax.shard_map(
        body,
        mesh=mesh,
        in_specs=(
            P(("grp", "tm"), None),
            P("tm", None),
            P(("grp", "tm"), None),
            P("tm", None),
            P(("grp", "tm"), None, None),
            P(("grp", "tm")),
            P(("grp", "tm")),
            P(("grp", "tm")),
            P(("grp", "tm"), None),
            P(),
            P(),
        ),
        out_specs=(P(("grp", "tm"), None), P("tm", None), P(("grp", "tm"), None), P("tm", None)),
        check_vma=False,
    )
```

time: 47.4 us -> 43.1 us (0.909)
  the two profiles are of different devices: /device:TPU:1 before, /device:TPU:31 now
where the time goes in v2:
time: 43.1 us; the launch traced here: 42.8 us
  Pallas kernels  41.5 us (96%)
  between operations  1.29 us (3%)
    pallas_call x1, Pallas kernels, body(): pl.pallas_call(kernel, name='pdhg', out_shape=(jax.ShapeDtypeStruct((ITER...  40.1 us
    pallas_call x1, Pallas kernels, body(): pl.pallas_call(means, name='means', out_shape=(columns, rows, columns, ro...  1.4 us

profile of v2, /device:TPU:31, one launch (start us, length us, event | category | flops | bytes accessed | tf_op | source)
XLA Modules:
  0.0 42.8 jit_solution(3723205524570860070)
XLA Ops:
  1.3 40.1 %pdhg.1 = (f32[2,16,128]{2,1,0:T(8,128)}, f32[2,4,8,128]{3,2,1,0:T(8,128)}) custom-call(f32[16,128]{1,0:T(8,128)} %x_hbm.1, f32[4,8,128]{2,1,0:T(8,128)} %bitcast.8, f32[16,128]{1,0:T(8,128)} %cost_hbm.1, f32[4,8,128]{2,1,0:T(8,128)} %bitcast.9, f32[64,128,128]{2,1,0:T(8,128)} %tiles_hbm.1, s32[64]{0:T(128)} %cols_hbm.1, s32[1]{0:T(128)S(6)} %copy.15.count_hbm, ...), custom_call_target="tpu_custom_call" | custom-call | tf_op jit(solution)/shard_map/pdhg/pallas_call | solution.py:571
  41.4 1.4 %means.1 = (f32[16,128]{1,0:T(8,128)}, f32[32,128]{1,0:T(8,128)}, f32[16,128]{1,0:T(8,128)}, f32[32,128]{1,0:T(8,128)}) custom-call(f32[2,16,128]{2,1,0:T(8,128)} %get-tuple-element.6.primals_ref, f32[2,32,128]{2,1,0:T(8,128)} %bitcast.7), custom_call_target="tpu_custom_call" | custom-call | tf_op jit(solution)/shard_map/means/pallas_call | solution.py:636

commit v3 on v2

--- a/solution.py
+++ b/solution.py
@@ -15,10 +15,13 @@
 TILE = 128
 CB = 16
 RB = 32
-OWN = 4
+OWN = 2
 PIECE = RB // OWN
 WIN = 3 * RB
 CHUNK = 8
+AM = 24
+FM = 16
+HALVED = max(AM, FM)
 
 LAST, NEXT = 15, 16
 SLOT_ROWS = 6 * PIECE
@@ -58,9 +61,14 @@
     staged,
     turned,
     factors,
-    select,
+    weights,
+    placed,
+    product,
+    select_f,
+    select_a,
     partial,
     pick,
+    pick_last,
     window_y,
     window_rhs,
     window_next,
@@ -84,7 +92,9 @@
     time = lax.axis_index("tm")
     place = group // 2
     core = lax.rem(group, 2)
-    is_owner = core == 1
+    on_core = core == 1
+    is_owner = on_core & ((place == 1) | (place == 2))
+    mine = place // 2
 
     def at(distance):
         return time + distance
@@ -97,7 +107,10 @@
         return sum(jnp.where(exists(distance), 1, 0) for distance in distances)
 
     def owner(offset):
-        return lax.rem(place + offset, OWN)
+        return lax.rem(mine + offset, OWN)
+
+    def owner_group(offset):
+        return 2 * owner(offset) + 3
 
     def far(distance):
         return (time == LAST) if distance > 0 else (time == NEXT)
@@ -125,10 +138,12 @@
         )
 
     def greet_all(distance):
-        for offset in (3, 2, 1, 0):
+        for offset in range(7, -1, -1):
             if distance or offset:
-                greet(2 * owner(offset) + 1, at(distance))
-            greet(2 * owner(offset), at(distance))
+                greet(lax.rem(group + offset, 8), at(distance))
+
+    source_place = jnp.where(place >= 2, 0, 3)
+    left = jnp.where(place == 3, 0, 2)
 
     @pl.when(is_owner)
     def _():
@@ -144,17 +159,25 @@
     def _():
         for distance in (1, -1):
 
-            @pl.when(far(distance))
-            def _():
-                greet(2 * jnp.where(place >= 2, 0, 3) + 1, at(distance))
+            @pl.when(on_core & far(distance))
+            def _():
+                greet(2 * source_place + 1, at(distance))
+
+            @pl.when(on_core & near(distance))
+            def _():
+                greet(group, at(distance))
 
             @pl.when(near(distance))
             def _():
                 for offset in range(OWN):
-                    greet(2 * owner(offset) + 1, at(distance))
+                    greet(owner_group(offset), at(distance))
 
         for offset in range(OWN):
-            greet(2 * owner(offset) + 1, time)
+            greet(owner_group(offset), time)
+
+        @pl.when(jnp.logical_not(on_core) & at_end)
+        def _():
+            greet(group + 1, time)
 
     inputs = []
     for index, (source, target) in enumerate(
@@ -187,16 +210,15 @@
     of_owner = 7
     for distance in (1, -1):
         of_owner = of_owner + jnp.where(near(distance), 8, 0)
-        of_owner = of_owner + jnp.where(far(distance), jnp.where(at_end, 6, 4), 0)
+        of_owner = of_owner + jnp.where(far(distance), OWN, 0)
     two_steps = jnp.where((time == LAST - 1) | (time == NEXT + 1), OWN, 0)
     of_other = OWN * number((1, 0, -1))
-    pl.semaphore_wait(barrier, jnp.where(is_owner, of_owner, of_other) + two_steps)
+    of_sender = of_other + number((1, -1)) + 1
+    peers = jnp.where(is_owner, of_owner, jnp.where(on_core, of_sender, of_other))
+    pl.semaphore_wait(barrier, peers + two_steps)
 
     def dual_copies(distance):
         slot = 1 - distance
-        crossing = far(distance)
-        first = jnp.where(crossing, jnp.where(place == 3, 0, 2), place)
-        second = lax.rem(first + 1, 4)
 
         def copy(target, number):
             return pltpu.make_async_remote_copy(
@@ -204,20 +226,30 @@
                 dst_ref=window_y.at[:, slot],
                 send_sem=dual_sems.at[slot // 2 * 4 + number],
                 recv_sem=halo_sems.at[slot],
-                device_id=(target, at(distance)),
+                device_id=(2 * target + 1, at(distance)),
                 device_id_type=MESH,
             )
 
-        pairs = [
-            (is_owner & exists(distance) & (jnp.logical_not(crossing) | at_end), [copy(2 * first, 0), copy(2 * first + 1, 1)]),
-            (is_owner & crossing & at_end, [copy(2 * second, 2), copy(2 * second + 1, 3)]),
+        return [
+            (on_core & far(distance) & at_end, [copy(left, 0), copy(left + 1, 1)]),
+            (on_core & near(distance), [copy(place, 2)]),
         ]
-        return pairs
+
+    def pass_on(distance):
+        slot = 1 + distance
+        return pltpu.make_async_remote_copy(
+            src_ref=window_y.at[:, slot],
+            dst_ref=window_y.at[:, slot],
+            send_sem=dual_sems.at[slot // 2 * 4 + 3],
+            recv_sem=halo_sems.at[slot],
+            device_id=(group - 1, time),
+            device_id_type=MESH,
+        )
 
     def rhs_copy(distance):
         slot = 1 - distance
         return pltpu.make_async_remote_copy(
-            src_ref=rhs_ref.at[place],
+            src_ref=rhs_ref.at[mine],
             dst_ref=window_rhs.at[slot],
             send_sem=halo_sems.at[slot + 4],
             recv_sem=halo_sems.at[slot + 1],
@@ -242,7 +274,7 @@
                 rhs_copy(distance).start()
 
     window_y[:, 1] = y_ref[...]
-    window_rhs[1] = rhs_ref[place]
+    window_rhs[1] = rhs_ref[mine]
 
     for chunk in range(NT // CHUNK):
         loads[chunk].wait()
@@ -251,7 +283,18 @@
             turned[slot] = staged[slot].T
             return carry
 
-        lax.fori_loop(chunk * CHUNK, (chunk + 1) * CHUNK, turn, 0, unroll=4)
+        if chunk * CHUNK < NT - FM:
+            lax.fori_loop(chunk * CHUNK, (chunk + 1) * CHUNK, turn, 0, unroll=4)
+
+        def halve(slot, carry):
+            high, low = split(staged[slot])
+            base = pl.multiple_of((slot - (NT - HALVED)) * TILE, TILE)
+            weights[pl.ds(base, TILE), 0:TILE] = high
+            weights[pl.ds(base, TILE), TILE : 2 * TILE] = low
+            return carry
+
+        if chunk * CHUNK >= NT - HALVED:
+            lax.fori_loop(chunk * CHUNK, (chunk + 1) * CHUNK, halve, 0, unroll=4)
 
     var_class = class_ref[...]
     lower = jnp.zeros((CB, TILE), F32)
@@ -272,38 +315,90 @@
     scatter = jnp.where(scatter, 1.0, 0.0)
     chosen = jnp.concatenate([scatter, jnp.where(gather, 1.0, 0.0)], axis=0)
     pick[...] = jnp.concatenate([scatter, scatter], axis=0).astype(BF16)
-    spread = lax.broadcasted_iota(jnp.int32, (NT, 8 * NT), 1) // 8 == lax.broadcasted_iota(jnp.int32, (NT, 8 * NT), 0)
-    chosen = jnp.dot(chosen.astype(BF16), jnp.where(spread, 1.0, 0.0).astype(BF16), preferred_element_type=F32)
+    if AM:
+        last = scatter.T[NT - AM :]
+        pick_last[...] = jnp.concatenate([last, last], axis=1).astype(BF16)
     chosen = chosen.astype(BF16)
-    select[...] = jnp.concatenate([chosen, chosen], axis=1)
-
-    def add_up(first, last):
-        high, low = split(partial[...])
-        return jnp.dot(
-            select[first:last], jnp.concatenate([high, low], axis=0), preferred_element_type=F32
-        )
+
+    def spread(alone):
+        width = 8 * (NT - alone) + alone
+        lane = lax.broadcasted_iota(jnp.int32, (NT, width), 1)
+        owner_slot = jnp.where(lane < 8 * (NT - alone), lane // 8, lane - 7 * (NT - alone))
+        hit = owner_slot == lax.broadcasted_iota(jnp.int32, (NT, width), 0)
+        return jnp.where(hit, 1.0, 0.0).astype(BF16)
+
+    def twice(value):
+        value = value.astype(BF16)
+        return jnp.concatenate([value, value], axis=1)
+
+    select_f[...] = twice(jnp.dot(chosen[:WIN], spread(FM), preferred_element_type=F32))
+    select_a[...] = twice(
+        jnp.dot(chosen[WIN:], spread(0)[:, : 8 * (NT - AM)], preferred_element_type=F32)
+    )
+
+    def add_up(select, values):
+        high, low = split(values)
+        return jnp.dot(select, jnp.concatenate([high, low], axis=0), preferred_element_type=F32)
 
     def fold(value):
         return jnp.sum(value.reshape(TILE // 8, 8, TILE), axis=0)
 
+    sub_id = lax.broadcasted_iota(jnp.int32, (CB, TILE), 0)
+
     def adjoint(field):
-        high, low = split(field[...].reshape(WIN, TILE).T)
+        field = field[...].reshape(WIN, TILE)
+        high, low = split(field.T)
         columns = jnp.dot(
             jnp.concatenate([high, low], axis=1), pick[...], preferred_element_type=F32
         )
-        for slot in range(NT):
+        if AM:
+            high, low = split(field)
+            rows = lax.dot_general(
+                pick_last[...],
+                jnp.concatenate([high, low], axis=0),
+                (((1,), (0,)), ((), ())),
+                preferred_element_type=F32,
+            )
+            for index in range(AM):
+                here = sub_id == cols_ref[NT - AM + index] - first_col
+                value = rows[index : index + 1]
+                high = value.astype(BF16).astype(F32)
+                span = slice(index * TILE, (index + 1) * TILE)
+                placed[0:CB, span] = jnp.where(here, high, 0.0).astype(BF16)
+                placed[CB : 2 * CB, span] = jnp.where(here, value - high, 0.0).astype(BF16)
+            total = jnp.dot(placed[...], weights[(HALVED - AM) * TILE :], preferred_element_type=F32)
+            total = total[:CB] + total[CB:]
+            total = total[:, :TILE] + total[:, TILE:]
+        for slot in range(NT - AM):
             factor = jnp.broadcast_to(columns[:, slot : slot + 1], (TILE, TILE))
             partial[8 * slot : 8 * slot + 8] = fold(staged[slot] * factor)
-        return add_up(WIN, WIN + CB)
+        rest = add_up(select_a[...], partial[0 : 8 * (NT - AM)])
+        return total + rest if AM else rest
 
     def forward(field):
+        if FM:
+            high, low = split(field)
+            halves = jnp.concatenate([high, low], axis=0)
+            result = lax.dot_general(
+                jnp.concatenate([halves, halves], axis=1),
+                weights[(HALVED - FM) * TILE :],
+                (((1,), (1,)), ((), ())),
+                preferred_element_type=F32,
+            )
+            for index in range(FM):
+                span = slice(index * TILE, (index + 1) * TILE)
+                product[index] = result[:CB, span] + result[CB:, span]
         columns = field.T
         for block in range(CB):
             factors[block] = jnp.broadcast_to(columns[:, block : block + 1], (TILE, TILE))
-        for slot in range(NT):
+        for slot in range(NT - FM):
             col = jnp.clip(cols_ref[slot] - first_col, 0, CB - 1)
             partial[8 * slot : 8 * slot + 8] = fold(turned[slot] * factors[col])
-        return add_up(0, WIN)
+        for index in range(FM):
+            col = jnp.clip(cols_ref[NT - FM + index] - first_col, 0, CB - 1)
+            row = 8 * (NT - FM) + index
+            partial[row : row + 1] = product[index, pl.ds(col, 1), :]
+        return add_up(select_f[...], partial[0 : 8 * (NT - FM) + FM])
 
     def primal_update(primal, adjoint_part):
         moved = primal - STEP * (cost_ref[...] - adjoint_part)
@@ -315,7 +410,7 @@
             dst_ref=target,
             send_sem=sums_sent.at[sems, distance + 2],
             recv_sem=sums_recv.at[sems, 2 - distance],
-            device_id=(2 * owner(offset) + 1, at(distance)),
+            device_id=(owner_group(offset), at(distance)),
             device_id_type=MESH,
         )
 
@@ -355,7 +450,7 @@
         return to_owner(source, target, distance, offset, 1)
 
     def to_owners(distance, copy):
-        for offset in (3, 2, 1, 0):
+        for offset in (1, 0):
             if distance or offset:
                 copy(distance, offset).start()
             else:
@@ -394,12 +489,16 @@
             def _():
                 wait_rows(semaphores.at[1, distance + 2], copies if distance else own)
 
-    for distance in (1, -1):
-
-        @pl.when(exists(distance))
+    for distance, when in ((1, near(1)), (-1, near(-1)), (1, far(1)), (-1, far(-1))):
+
+        @pl.when(when)
         def _():
             dual_in = window_y.at[:, 1 + distance]
             pltpu.make_async_copy(dual_in, dual_in, halo_sems.at[1 + distance]).wait()
+
+            @pl.when(on_core)
+            def _():
+                pass_on(distance).start()
 
     primal_0 = x_ref[...]
     primal_1 = primal_update(primal_0, adjoint(window_y))
@@ -423,7 +522,7 @@
             @pl.when(when)
             def _():
                 block = jnp.where(time == NEXT, 0, 1) if pieces == 2 else 1
-                source = pl.ds(pl.multiple_of((place * 3 + block) * PIECE, 8), pieces * PIECE)
+                source = pl.ds(pl.multiple_of((mine * 3 + block) * PIECE, 8), pieces * PIECE)
                 target = pl.ds(pl.multiple_of(group * SLOT_ROWS, 8), pieces * PIECE)
                 parts_a[target] = terms_a[source]
 
@@ -436,35 +535,36 @@
 
         wait_sums_a(sums_recv, ((2, time == LAST), (-2, time == NEXT)), 8, 7)
         sums = jnp.sum(parts_a[...].reshape(8, SLOT_ROWS, TILE), axis=0)
-        low = sums[0:8] + sums[16:24]
-        high = sums[8:16] + sums[24:32]
+        step = [sums[index * PIECE : (index + 1) * PIECE] for index in range(6)]
+        low = step[0] + step[2]
+        high = step[1] + step[3]
         upper_side = time == NEXT
-        first = jnp.where(upper_side, high, low) + sums[32:40]
-        second = jnp.where(upper_side, low, high) + sums[40:48]
+        first = jnp.where(upper_side, high, low) + step[4]
+        second = jnp.where(upper_side, low, high) + step[5]
         for block in range(3):
             image = first if block == 1 else second
-            piece_a[block] = jnp.maximum(window_y[place, block] + STEP * (window_rhs[block] - image), 0.0)
+            piece_a[block] = jnp.maximum(window_y[mine, block] + STEP * (window_rhs[block] - image), 0.0)
         for distance in (1, -1):
 
             @pl.when(near(distance))
             def _():
                 for offset in range(7, -1, -1):
                     from_owner(
-                        piece_a.at[1], window_next.at[place, 1 - distance], offset, distance, 2 + distance
+                        piece_a.at[1], window_next.at[mine, 1 - distance], offset, distance, 2 + distance
                     ).start()
 
         @pl.when(edge)
         def _():
             span = pl.ds(jnp.where(time == NEXT, 0, 1), 2)
             for offset in range(7, 0, -1):
-                from_owner(piece_a.at[span], window_next.at[place, span], offset, 0, 0).start()
-            window_next[place, span] = piece_a[span]
+                from_owner(piece_a.at[span], window_next.at[mine, span], offset, 0, 0).start()
+            window_next[mine, span] = piece_a[span]
 
         @pl.when(jnp.logical_not(edge))
         def _():
             for offset in range(7, 0, -1):
-                from_owner(piece_a.at[1], window_next.at[place, 1], offset, 0, 0).start()
-            window_next[place, 1] = piece_a[1]
+                from_owner(piece_a.at[1], window_next.at[mine, 1], offset, 0, 0).start()
+            window_next[mine, 1] = piece_a[1]
 
     for owned, others in ((is_owner, OWN - 1), (jnp.logical_not(is_owner), OWN)):
         for pieces, when in ((2, edge), (1, jnp.logical_not(edge))):
@@ -493,15 +593,15 @@
 
     @pl.when(is_owner)
     def _():
-        own = pl.ds(pl.multiple_of(place * 3 * PIECE + PIECE, 8), PIECE)
+        own = pl.ds(pl.multiple_of(mine * 3 * PIECE + PIECE, 8), PIECE)
         parts_b[pl.ds(pl.multiple_of(group * 3 * PIECE + PIECE, 8), PIECE)] = terms_b[own]
         wait_sums_b(sums_recv, 8, 7)
         sums = jnp.sum(parts_b[...].reshape(8, 3 * PIECE, TILE), axis=0)
-        image = sums[0:8] + sums[8:16] + sums[16:24]
+        image = sums[0:PIECE] + sums[PIECE : 2 * PIECE] + sums[2 * PIECE :]
         piece_b[...] = jnp.maximum(piece_a[1] + STEP * (window_rhs[1] - image), 0.0)
         for offset in range(7, 0, -1):
-            from_owner(piece_b, last_dual.at[place], offset, 0, 2).start()
-        last_dual[place] = piece_b[...]
+            from_owner(piece_b, last_dual.at[mine], offset, 0, 2).start()
+        last_dual[mine] = piece_b[...]
         wait_rows(recv_sems.at[2], OWN - 1)
 
     @pl.when(jnp.logical_not(is_owner))
@@ -517,6 +617,12 @@
             def _():
                 for copy in copies:
                     copy.wait_send()
+
+    for distance in (1, -1):
+
+        @pl.when(on_core & exists(distance))
+        def _():
+            pass_on(distance).wait_send()
 
     two_steps = ((2, time == LAST - 1), (-2, time == NEXT + 1))
 
@@ -592,9 +698,14 @@
             pltpu.VMEM((NT, TILE, TILE), F32),
             pltpu.VMEM((NT, TILE, TILE), F32),
             pltpu.VMEM((CB, TILE, TILE), F32),
-            pltpu.VMEM((WIN + CB, 16 * NT), BF16),
+            pltpu.VMEM((max(HALVED, 1) * TILE, 2 * TILE), BF16),
+            pltpu.VMEM((2 * CB, max(AM, 1) * TILE), BF16),
+            pltpu.VMEM((max(FM, 1), CB, TILE), F32),
+            pltpu.VMEM((WIN, 16 * (NT - FM) + 2 * FM), BF16),
+            pltpu.VMEM((CB, 16 * (NT - AM)), BF16),
             pltpu.VMEM((8 * NT, TILE), F32),
             pltpu.VMEM((2 * WIN, NT), BF16),
+            pltpu.VMEM((max(AM, 1), 2 * WIN), BF16),
             pltpu.VMEM((OWN, 3, PIECE, TILE), F32),
             pltpu.VMEM((3, PIECE, TILE), F32),
             pltpu.VMEM((OWN, 3, PIECE, TILE), F32),

time: 43.1 us -> 40.6 us (0.942)
  Pallas kernels: 41.5 us -> 38.9 us
    pallas_call x1, Pallas kernels: 40.1 us -> 37.5 us  [body(): pl.pallas_call(kernel, name='pdhg', out_shape=(jax.ShapeDtypeStruct((ITER...]
where the time goes in v3:
time: 40.6 us; the launch traced here: 40.2 us
  Pallas kernels  38.9 us (96%)
  between operations  1.29 us (3%)
    pallas_call x1, Pallas kernels, body(): pl.pallas_call(kernel, name='pdhg', out_shape=(jax.ShapeDtypeStruct((ITER...  37.5 us
    pallas_call x1, Pallas kernels, body(): pl.pallas_call(means, name='means', out_shape=(columns, rows, columns, ro...  1.4 us

profile of v3, /device:TPU:31, one launch (start us, length us, event | category | flops | bytes accessed | tf_op | source)
XLA Modules:
  0.0 40.2 jit_solution(14901727985054753593)
XLA Ops:
  1.3 37.5 %pdhg.1 = (f32[2,16,128]{2,1,0:T(8,128)}, f32[2,2,16,128]{3,2,1,0:T(8,128)}) custom-call(f32[16,128]{1,0:T(8,128)} %x_hbm.1, f32[2,16,128]{2,1,0:T(8,128)} %bitcast.8, f32[16,128]{1,0:T(8,128)} %cost_hbm.1, f32[2,16,128]{2,1,0:T(8,128)} %bitcast.9, f32[64,128,128]{2,1,0:T(8,128)} %tiles_hbm.1, s32[64]{0:T(128)} %cols_hbm.1, s32[1]{0:T(128)S(6)} %copy.15.count_hbm, ...), custom_call_target="tpu_custom_call" | custom-call | tf_op jit(solution)/shard_map/pdhg/pallas_call | solution.py:677
  38.8 1.4 %means.1 = (f32[16,128]{1,0:T(8,128)}, f32[32,128]{1,0:T(8,128)}, f32[16,128]{1,0:T(8,128)}, f32[32,128]{1,0:T(8,128)}) custom-call(f32[2,16,128]{2,1,0:T(8,128)} %get-tuple-element.6.primals_ref, f32[2,32,128]{2,1,0:T(8,128)} %bitcast.7), custom_call_target="tpu_custom_call" | custom-call | tf_op jit(solution)/shard_map/means/pallas_call | solution.py:747

commit v4 on v3

--- a/solution.py
+++ b/solution.py
@@ -124,11 +124,17 @@
     def both(distance):
         return edge if distance == 0 else far(distance)
 
-    parts_a[...] = jnp.zeros_like(parts_a)
-    parts_b[...] = jnp.zeros_like(parts_b)
-    window_y[...] = jnp.zeros_like(window_y)
-    window_next[...] = jnp.zeros_like(window_next)
     window_rhs[...] = jnp.zeros_like(window_rhs)
+
+    @pl.when(jnp.logical_not(edge))
+    def _():
+        parts_a[...] = jnp.zeros_like(parts_a)
+
+    @pl.when((time == 0) | (time == 31))
+    def _():
+        parts_b[...] = jnp.zeros_like(parts_b)
+        window_y[...] = jnp.zeros_like(window_y)
+        window_next[...] = jnp.zeros_like(window_next)
 
     barrier = pltpu.get_barrier_semaphore()
 
@@ -526,16 +532,33 @@
                 target = pl.ds(pl.multiple_of(group * SLOT_ROWS, 8), pieces * PIECE)
                 parts_a[target] = terms_a[source]
 
+        def summed(ref, stride, first):
+            return sum(
+                ref[pl.ds(pl.multiple_of((index * stride + first) * PIECE, PIECE), PIECE)] for index in range(8)
+            )
+
+        for distance, when, pieces in steps_a():
+
+            @pl.when(when & jnp.logical_not(far(distance) if distance else False))
+            def _():
+                wait_rows(sums_recv.at[0, distance + 2], pieces * (8 if distance else 7))
+
+        early = [summed(parts_a, 6, index) for index in (0, 1, 4)]
         for distance in (1, -1):
 
             @pl.when(far(distance))
             def _():
                 rhs_in = window_rhs.at[1 + distance]
                 pltpu.make_async_copy(rhs_in, rhs_in, halo_sems.at[2 + distance]).wait()
-
-        wait_sums_a(sums_recv, ((2, time == LAST), (-2, time == NEXT)), 8, 7)
-        sums = jnp.sum(parts_a[...].reshape(8, SLOT_ROWS, TILE), axis=0)
-        step = [sums[index * PIECE : (index + 1) * PIECE] for index in range(6)]
+                wait_rows(sums_recv.at[0, distance + 2], 2 * 8)
+
+        for distance, when in ((2, time == LAST), (-2, time == NEXT)):
+
+            @pl.when(when)
+            def _():
+                wait_rows(sums_recv.at[0, distance + 2], 8)
+
+        step = [early[0], early[1], summed(parts_a, 6, 2), summed(parts_a, 6, 3), early[2], summed(parts_a, 6, 5)]
         low = step[0] + step[2]
         high = step[1] + step[3]
         upper_side = time == NEXT
@@ -544,6 +567,19 @@
         for block in range(3):
             image = first if block == 1 else second
             piece_a[block] = jnp.maximum(window_y[mine, block] + STEP * (window_rhs[block] - image), 0.0)
+        @pl.when(edge)
+        def _():
+            span = pl.ds(jnp.where(time == NEXT, 0, 1), 2)
+            for offset in (3, 5, 1, 7, 4, 2, 6):
+                from_owner(piece_a.at[span], window_next.at[mine, span], offset, 0, 0).start()
+            window_next[mine, span] = piece_a[span]
+
+        @pl.when(jnp.logical_not(edge))
+        def _():
+            for offset in (3, 5, 1, 7, 4, 2, 6):
+                from_owner(piece_a.at[1], window_next.at[mine, 1], offset, 0, 0).start()
+            window_next[mine, 1] = piece_a[1]
+
         for distance in (1, -1):
 
             @pl.when(near(distance))
@@ -553,19 +589,6 @@
                         piece_a.at[1], window_next.at[mine, 1 - distance], offset, distance, 2 + distance
                     ).start()
 
-        @pl.when(edge)
-        def _():
-            span = pl.ds(jnp.where(time == NEXT, 0, 1), 2)
-            for offset in range(7, 0, -1):
-                from_owner(piece_a.at[span], window_next.at[mine, span], offset, 0, 0).start()
-            window_next[mine, span] = piece_a[span]
-
-        @pl.when(jnp.logical_not(edge))
-        def _():
-            for offset in range(7, 0, -1):
-                from_owner(piece_a.at[1], window_next.at[mine, 1], offset, 0, 0).start()
-            window_next[mine, 1] = piece_a[1]
-
     for owned, others in ((is_owner, OWN - 1), (jnp.logical_not(is_owner), OWN)):
         for pieces, when in ((2, edge), (1, jnp.logical_not(edge))):
 
@@ -595,11 +618,29 @@
     def _():
         own = pl.ds(pl.multiple_of(mine * 3 * PIECE + PIECE, 8), PIECE)
         parts_b[pl.ds(pl.multiple_of(group * 3 * PIECE + PIECE, 8), PIECE)] = terms_b[own]
-        wait_sums_b(sums_recv, 8, 7)
-        sums = jnp.sum(parts_b[...].reshape(8, 3 * PIECE, TILE), axis=0)
-        image = sums[0:PIECE] + sums[PIECE : 2 * PIECE] + sums[2 * PIECE :]
+        def summed(first):
+            return sum(
+                parts_b[pl.ds(pl.multiple_of((index * 3 + first) * PIECE, PIECE), PIECE)] for index in range(8)
+            )
+
+        wait_rows(sums_recv.at[1, 2], 7)
+        for distance in (1, -1):
+
+            @pl.when(near(distance))
+            def _():
+                wait_rows(sums_recv.at[1, distance + 2], 8)
+
+        near_block = jnp.where(time == LAST, 0, 2)
+        early = summed(1) + summed(near_block)
+        for distance in (1, -1):
+
+            @pl.when(far(distance))
+            def _():
+                wait_rows(sums_recv.at[1, distance + 2], 8)
+
+        image = early + summed(2 - near_block)
         piece_b[...] = jnp.maximum(piece_a[1] + STEP * (window_rhs[1] - image), 0.0)
-        for offset in range(7, 0, -1):
+        for offset in (3, 5, 1, 7, 4, 2, 6):
             from_owner(piece_b, last_dual.at[mine], offset, 0, 2).start()
         last_dual[mine] = piece_b[...]
         wait_rows(recv_sems.at[2], OWN - 1)

time: 40.6 us -> 39.8 us (0.980)
  Pallas kernels: 38.9 us -> 38.3 us
    pallas_call x1, Pallas kernels: 37.5 us -> 36.9 us  [body(): pl.pallas_call(kernel, name='pdhg', out_shape=(jax.ShapeDtypeStruct((ITER...]
where the time goes in v4:
time: 39.8 us; the launch traced here: 39.6 us
  Pallas kernels  38.3 us (96%)
  between operations  1.29 us (3%)
    pallas_call x1, Pallas kernels, body(): pl.pallas_call(kernel, name='pdhg', out_shape=(jax.ShapeDtypeStruct((ITER...  36.9 us
    pallas_call x1, Pallas kernels, body(): pl.pallas_call(means, name='means', out_shape=(columns, rows, columns, ro...  1.4 us

profile of v4, /device:TPU:31, one launch (start us, length us, event | category | flops | bytes accessed | tf_op | source)
XLA Modules:
  0.0 39.6 jit_solution(3933074471233496490)
XLA Ops:
  1.3 36.9 %pdhg.1 = (f32[2,16,128]{2,1,0:T(8,128)}, f32[2,2,16,128]{3,2,1,0:T(8,128)}) custom-call(f32[16,128]{1,0:T(8,128)} %x_hbm.1, f32[2,16,128]{2,1,0:T(8,128)} %bitcast.8, f32[16,128]{1,0:T(8,128)} %cost_hbm.1, f32[2,16,128]{2,1,0:T(8,128)} %bitcast.9, f32[64,128,128]{2,1,0:T(8,128)} %tiles_hbm.1, s32[64]{0:T(128)} %cols_hbm.1, s32[1]{0:T(128)S(6)} %copy.15.count_hbm, ...), custom_call_target="tpu_custom_call" | custom-call | tf_op jit(solution)/shard_map/pdhg/pallas_call | solution.py:718
  38.2 1.4 %means.1 = (f32[16,128]{1,0:T(8,128)}, f32[32,128]{1,0:T(8,128)}, f32[16,128]{1,0:T(8,128)}, f32[32,128]{1,0:T(8,128)}) custom-call(f32[2,16,128]{2,1,0:T(8,128)} %get-tuple-element.6.primals_ref, f32[2,32,128]{2,1,0:T(8,128)} %bitcast.7), custom_call_target="tpu_custom_call" | custom-call | tf_op jit(solution)/shard_map/means/pallas_call | solution.py:788

commit v5 on v4

--- a/solution.py
+++ b/solution.py
@@ -78,8 +78,9 @@
     parts_b,
     piece_a,
     piece_b,
-    last_dual,
+    primals,
     load_sem,
+    out_sems,
     input_sems,
     dual_sems,
     halo_sems,
@@ -397,9 +398,13 @@
         columns = field.T
         for block in range(CB):
             factors[block] = jnp.broadcast_to(columns[:, block : block + 1], (TILE, TILE))
-        for slot in range(NT - FM):
+
+        def product_of(slot, carry):
             col = jnp.clip(cols_ref[slot] - first_col, 0, CB - 1)
-            partial[8 * slot : 8 * slot + 8] = fold(turned[slot] * factors[col])
+            partial[pl.ds(pl.multiple_of(8 * slot, 8), 8)] = fold(turned[slot] * factors[col])
+            return carry
+
+        lax.fori_loop(0, NT - FM, product_of, 0, unroll=16)
         for index in range(FM):
             col = jnp.clip(cols_ref[NT - FM + index] - first_col, 0, CB - 1)
             row = 8 * (NT - FM) + index
@@ -610,9 +615,15 @@
         def _():
             to_owners(distance, copy_b)
 
-    primal_out[0] = primal_1
-    primal_out[1] = primal_2
-    dual_out[0] = window_next[:, 1]
+    primals[0] = primal_1
+    primals[1] = primal_2
+    results = [
+        pltpu.make_async_copy(primals, primal_out, out_sems.at[0]),
+        pltpu.make_async_copy(window_next.at[:, 1], dual_out.at[0], out_sems.at[1]),
+    ]
+    for copy in results:
+        copy.start()
+
 
     @pl.when(is_owner)
     def _():
@@ -641,15 +652,18 @@
         image = early + summed(2 - near_block)
         piece_b[...] = jnp.maximum(piece_a[1] + STEP * (window_rhs[1] - image), 0.0)
         for offset in (3, 5, 1, 7, 4, 2, 6):
-            from_owner(piece_b, last_dual.at[mine], offset, 0, 2).start()
-        last_dual[mine] = piece_b[...]
+            from_owner(piece_b, dual_out.at[1, mine], offset, 0, 2).start()
+        own_copy = pltpu.make_async_copy(piece_b, dual_out.at[1, mine], out_sems.at[2])
+        own_copy.start()
         wait_rows(recv_sems.at[2], OWN - 1)
+        own_copy.wait()
 
     @pl.when(jnp.logical_not(is_owner))
     def _():
         wait_rows(recv_sems.at[2], OWN)
 
-    dual_out[1] = last_dual[...]
+    for copy in results:
+        copy.wait()
 
     for distance in (1, -1):
         for when, copies in dual_copies(distance):
@@ -723,7 +737,7 @@
             jax.ShapeDtypeStruct((ITERS, OWN, PIECE, TILE), F32),
         ),
         in_specs=[pl.BlockSpec(memory_space=pltpu.HBM)] * 12,
-        out_specs=(vmem, vmem),
+        out_specs=(pl.BlockSpec(memory_space=pl.ANY),) * 2,
         scratch_shapes=[
             pltpu.VMEM((CB, TILE), F32),
             pltpu.VMEM((OWN, PIECE, TILE), F32),
@@ -756,8 +770,9 @@
             pltpu.VMEM((8 * 3 * PIECE, TILE), F32),
             pltpu.VMEM((3, PIECE, TILE), F32),
             pltpu.VMEM((PIECE, TILE), F32),
-            pltpu.VMEM((OWN, PIECE, TILE), F32),
+            pltpu.VMEM((ITERS, CB, TILE), F32),
             pltpu.SemaphoreType.DMA((NT // CHUNK,)),
+            pltpu.SemaphoreType.DMA((3,)),
             pltpu.SemaphoreType.DMA((11,)),
             pltpu.SemaphoreType.DMA((8,)),
             pltpu.SemaphoreType.DMA((8,)),

time: 39.8 us -> 39.1 us (0.982)
  Pallas kernels: 38.3 us -> 37.6 us
    pallas_call x1, Pallas kernels: 36.9 us -> 36.2 us  [body(): pl.pallas_call(kernel, name='pdhg', out_shape=(jax.ShapeDtypeStruct((ITER...]
where the time goes in v5:
time: 39.1 us; the launch traced here: 38.8 us
  Pallas kernels  37.6 us (96%)
  between operations  1.29 us (3%)
    pallas_call x1, Pallas kernels, body(): pl.pallas_call(kernel, name='pdhg', out_shape=(jax.ShapeDtypeStruct((ITER...  36.2 us
    pallas_call x1, Pallas kernels, body(): pl.pallas_call(means, name='means', out_shape=(columns, rows, columns, ro...  1.4 us

profile of v5, /device:TPU:31, one launch (start us, length us, event | category | flops | bytes accessed | tf_op | source)
XLA Modules:
  0.0 38.8 jit_solution(242690365351708266)
XLA Ops:
  1.3 36.2 %pdhg.1 = (f32[2,16,128]{2,1,0:T(8,128)}, f32[2,2,16,128]{3,2,1,0:T(8,128)}) custom-call(f32[16,128]{1,0:T(8,128)} %x_hbm.1, f32[2,16,128]{2,1,0:T(8,128)} %bitcast.8, f32[16,128]{1,0:T(8,128)} %cost_hbm.1, f32[2,16,128]{2,1,0:T(8,128)} %bitcast.9, f32[64,128,128]{2,1,0:T(8,128)} %tiles_hbm.1, s32[64]{0:T(128)} %cols_hbm.1, s32[1]{0:T(128)S(6)} %copy.15.count_hbm, ...), custom_call_target="tpu_custom_call" | custom-call | tf_op jit(solution)/shard_map/pdhg/pallas_call | solution.py:732
  37.4 1.4 %means.1 = (f32[16,128]{1,0:T(8,128)}, f32[32,128]{1,0:T(8,128)}, f32[16,128]{1,0:T(8,128)}, f32[32,128]{1,0:T(8,128)}) custom-call(f32[2,16,128]{2,1,0:T(8,128)} %get-tuple-element.6.primals_ref, f32[2,32,128]{2,1,0:T(8,128)} %bitcast.7), custom_call_target="tpu_custom_call" | custom-call | tf_op jit(solution)/shard_map/means/pallas_call | solution.py:803

commit v6 on v5

--- a/solution.py
+++ b/solution.py
@@ -19,7 +19,7 @@
 PIECE = RB // OWN
 WIN = 3 * RB
 CHUNK = 8
-AM = 24
+AM = 40
 FM = 16
 HALVED = max(AM, FM)
 
@@ -609,9 +609,9 @@
 
     primal_2 = primal_update(primal_1, adjoint(window_next))
     terms_b[...] = forward(2.0 * primal_2 - primal_1)
-    for distance in (1, -1, 0):
-
-        @pl.when(exists(distance))
+    for distance, when in ((1, far(1)), (-1, far(-1)), (1, near(1)), (-1, near(-1)), (0, exists(0))):
+
+        @pl.when(when)
         def _():
             to_owners(distance, copy_b)
 

time: 39.1 us -> 38.7 us (0.990)
  Pallas kernels: 37.6 us -> 37.2 us
where the time goes in v6:
time: 38.7 us; the launch traced here: 38.5 us
  Pallas kernels  37.2 us (96%)
  between operations  1.29 us (3%)
    pallas_call x1, Pallas kernels, body(): pl.pallas_call(kernel, name='pdhg', out_shape=(jax.ShapeDtypeStruct((ITER...  35.8 us
    pallas_call x1, Pallas kernels, body(): pl.pallas_call(means, name='means', out_shape=(columns, rows, columns, ro...  1.4 us

profile of v6, /device:TPU:31, one launch (start us, length us, event | category | flops | bytes accessed | tf_op | source)
XLA Modules:
  0.0 38.5 jit_solution(7125767062281279658)
XLA Ops:
  1.3 35.8 %pdhg.1 = (f32[2,16,128]{2,1,0:T(8,128)}, f32[2,2,16,128]{3,2,1,0:T(8,128)}) custom-call(f32[16,128]{1,0:T(8,128)} %x_hbm.1, f32[2,16,128]{2,1,0:T(8,128)} %bitcast.8, f32[16,128]{1,0:T(8,128)} %cost_hbm.1, f32[2,16,128]{2,1,0:T(8,128)} %bitcast.9, f32[64,128,128]{2,1,0:T(8,128)} %tiles_hbm.1, s32[64]{0:T(128)} %cols_hbm.1, s32[1]{0:T(128)S(6)} %copy.15.count_hbm, ...), custom_call_target="tpu_custom_call" | custom-call | tf_op jit(solution)/shard_map/pdhg/pallas_call | solution.py:732
  37.1 1.4 %means.1 = (f32[16,128]{1,0:T(8,128)}, f32[32,128]{1,0:T(8,128)}, f32[16,128]{1,0:T(8,128)}, f32[32,128]{1,0:T(8,128)}) custom-call(f32[2,16,128]{2,1,0:T(8,128)} %get-tuple-element.6.primals_ref, f32[2,32,128]{2,1,0:T(8,128)} %bitcast.7), custom_call_target="tpu_custom_call" | custom-call | tf_op jit(solution)/shard_map/means/pallas_call | solution.py:803

commit v7 on v6

--- a/solution.py
+++ b/solution.py
@@ -19,7 +19,7 @@
 PIECE = RB // OWN
 WIN = 3 * RB
 CHUNK = 8
-AM = 40
+AM = 48
 FM = 16
 HALVED = max(AM, FM)
 

time: 38.7 us -> 38.8 us (level)
  no operation moved by 1% of the time
where the time goes in v7:
time: 38.8 us; the launch traced here: 38.5 us
  Pallas kernels  37.2 us (96%)
  between operations  1.29 us (3%)
    pallas_call x1, Pallas kernels, body(): pl.pallas_call(kernel, name='pdhg', out_shape=(jax.ShapeDtypeStruct((ITER...  35.8 us
    pallas_call x1, Pallas kernels, body(): pl.pallas_call(means, name='means', out_shape=(columns, rows, columns, ro...  1.4 us

profile of v7, /device:TPU:31, one launch (start us, length us, event | category | flops | bytes accessed | tf_op | source)
XLA Modules:
  0.0 38.5 jit_solution(4046231654831274401)
XLA Ops:
  1.3 35.8 %pdhg.1 = (f32[2,16,128]{2,1,0:T(8,128)}, f32[2,2,16,128]{3,2,1,0:T(8,128)}) custom-call(f32[16,128]{1,0:T(8,128)} %x_hbm.1, f32[2,16,128]{2,1,0:T(8,128)} %bitcast.8, f32[16,128]{1,0:T(8,128)} %cost_hbm.1, f32[2,16,128]{2,1,0:T(8,128)} %bitcast.9, f32[64,128,128]{2,1,0:T(8,128)} %tiles_hbm.1, s32[64]{0:T(128)} %cols_hbm.1, s32[1]{0:T(128)S(6)} %copy.15.count_hbm, ...), custom_call_target="tpu_custom_call" | custom-call | tf_op jit(solution)/shard_map/pdhg/pallas_call | solution.py:732
  37.1 1.4 %means.1 = (f32[16,128]{1,0:T(8,128)}, f32[32,128]{1,0:T(8,128)}, f32[16,128]{1,0:T(8,128)}, f32[32,128]{1,0:T(8,128)}) custom-call(f32[2,16,128]{2,1,0:T(8,128)} %get-tuple-element.6.primals_ref, f32[2,32,128]{2,1,0:T(8,128)} %bitcast.7), custom_call_target="tpu_custom_call" | custom-call | tf_op jit(solution)/shard_map/means/pallas_call | solution.py:803
